TPU v7x, 512 devices: a whole 4x8x8 slice. The times are simulated.
512 devices in a mesh: dp: 8 (over z), seq: 64 (over y, x, core).
Axes of the slice: x: 4, y: 8, z: 8, core: 2. Of those that a mesh axis runs over, the one named last changes fastest.
Arguments:
- frames_in: bfloat16 [8, 256, 2, 16, 32, 384], P('dp', 'seq'), may hold values from -6 to 6
- clip_frames: int32 [8, 32], P('dp'), may hold values from 1 to 21, 256 in all within a row
- res_ids: int32 [8, 32], P('dp'), may hold values from 0 to 1
- token_dest: int32 [8, 32768, 1], P('dp', 'seq'), may hold values from 0 to 511; in each aligned block of 512 rows (0 to 511, 512 to 1023, ..., all dimensions but the last counted through in order) at most 2 rows name the same one
- tconv_weight: bfloat16 [3, 384, 384], replicated, may hold values from -0.1875 to 0.1875
- tconv_bias: float32 [384], replicated, may hold values from -3 to 3
- head_gain: float32 [384], replicated, may hold values from 0.1 to 1.9
- head_weight: bfloat16 [3, 3, 3, 384, 16], replicated, may hold values from -0.0625 to 0.0625
- head_bias: float32 [16], replicated, may hold values from -3 to 3
- latent_mean: float32 [16], replicated, may hold values from -0.5 to 0.5
- latent_scale: float32 [16], replicated, may hold values from 0.5 to 2
Outputs:
- latent_slots: bfloat16 [8, 64, 512, 128], P('dp', 'seq')
Inputs may be any that keep to these rules, and one draw needn't show every extreme that they name: `clip_frames`: the 32 clips of a row fill its 256 latent frames exactly; some clip of each row has 21. `res_ids`: 0 marks a 480p clip, 1 a 720p clip. `token_dest`: among the 512 patches of one device no destination appears more than 2 times, a bound that some block reaches.
All inputs are finite; a program needn't handle non-finite values.
Results may differ from a plain program's by a relative error of at most 0.0055.
Values may be sent and summed in bfloat16 or wider, within the bound.
A program may use at most 64 MiB of HBM per device.

v0:
```python
import jax
import jax.numpy as jnp
from jax import lax
from jax.sharding import PartitionSpec as P


def from_behind(value, axis, steps):
    count = lax.axis_size(axis)
    first, last = (max(0, -steps), min(count, count - steps))
    return lax.ppermute(value, axis, [(source, source + steps) for source in range(first, last)])


def clip_lookup(lengths, resolution_ids, frame_index):
    clip_ends = jnp.cumsum(lengths)
    clip_starts = clip_ends - lengths
    belongs = (frame_index[:, None] >= clip_starts[None, :]) & (
        frame_index[:, None] < clip_ends[None, :]
    )
    clip_start = jnp.sum(jnp.where(belongs, clip_starts[None, :], 0), axis=1)
    resolution = jnp.sum(jnp.where(belongs, resolution_ids[None, :], 0), axis=1)
    return (clip_start, resolution)


def temporal_section(earlier, local_frames, tconv_weight, tconv_bias, first_mask):
    frame_count = local_frames.shape[0]
    height = local_frames.shape[2]
    columns = local_frames.shape[3]
    channels = local_frames.shape[4]
    temporal = jnp.dot(
        earlier.reshape(-1, channels), tconv_weight[0], preferred_element_type=jnp.float32
    )
    temporal = temporal + jnp.dot(
        local_frames[:, 0].reshape(-1, channels),
        tconv_weight[1],
        preferred_element_type=jnp.float32,
    )
    temporal = temporal + jnp.dot(
        local_frames[:, 1].reshape(-1, channels),
        tconv_weight[2],
        preferred_element_type=jnp.float32,
    )
    temporal = temporal.reshape(frame_count, height, columns, channels) + tconv_bias
    passed = local_frames[:, 1].astype(jnp.float32)
    return jnp.where(first_mask[:, None, None, None], passed, temporal).astype(jnp.bfloat16)


def activate(section_out, head_gain, picture_limit):
    columns = section_out.shape[2]
    values = section_out.astype(jnp.float32)
    mean_square = jnp.mean(values * values, axis=-1, keepdims=True)
    normalized = values * lax.rsqrt(mean_square + 1e-06) * head_gain
    inside = (jnp.arange(columns, dtype=jnp.int32)[None, :] < picture_limit[:, None]).astype(
        jnp.float32
    )
    activation = (jax.nn.silu(normalized) * inside[:, None, :, None]).astype(jnp.bfloat16)
    return (activation, inside)


def flat_taps(products, k, height, stride):
    span = height * stride
    running = jnp.zeros(products.shape[1:3] + (span,), jnp.float32)
    for a in range(3):
        for b in range(3):
            offset = a * stride + b
            running = running + products[(k * 3 + a) * 3 + b, :, :, offset : offset + span]
    return running


def on_device(
    frames_in,
    clip_frames,
    res_ids,
    token_dest,
    tconv_weight,
    tconv_bias,
    head_gain,
    head_weight,
    head_bias,
    latent_mean,
    latent_scale,
):
    local_frames = frames_in[0]
    frame_count = local_frames.shape[0]
    height = local_frames.shape[2]
    columns = local_frames.shape[3]
    channels = local_frames.shape[4]
    latent_dim = head_weight.shape[-1]
    stride = columns + 2
    first_frame = lax.axis_index("seq") * frame_count
    lengths = clip_frames[0]
    resolution_ids = res_ids[0]
    frame_index = first_frame + jnp.arange(frame_count, dtype=jnp.int32)
    clip_start, resolution = clip_lookup(lengths, resolution_ids, frame_index)
    picture_limit = jnp.where(resolution == 1, columns, columns * 13 // 20).astype(jnp.int32)
    carried = from_behind(local_frames[frame_count - 1, 1], "seq", 1)
    earlier = jnp.concatenate([carried[None], local_frames[: frame_count - 1, 1]], axis=0)
    section_out = temporal_section(
        earlier, local_frames, tconv_weight, tconv_bias, frame_index == clip_start
    )
    activation, inside = activate(section_out, head_gain, picture_limit)
    head_rows = jnp.transpose(head_weight, (0, 1, 2, 4, 3)).reshape(27 * latent_dim, channels)
    head_out = jnp.zeros((latent_dim, frame_count, height * stride), jnp.float32)
    received = from_behind(activation[frame_count - 2 :], "seq", 1)
    frames_act = jnp.concatenate([received, activation], axis=0)
    padded = jnp.pad(frames_act, ((0, 0), (1, 2), (1, 1), (0, 0)))
    products = lax.dot_general(
        head_rows,
        padded.reshape(-1, channels),
        (((1,), (1,)), ((), ())),
        preferred_element_type=jnp.float32,
    )
    products = products.reshape(27, latent_dim, frames_act.shape[0], (height + 3) * stride)
    for k in range(3):
        in_clip = (frame_index - 2 + k >= clip_start).astype(jnp.float32)
        head_out = (
            head_out
            + flat_taps(products[:, :, k : k + frame_count], k, height, stride)
            * in_clip[None, :, None]
        )
    head_out = head_out.reshape(latent_dim, frame_count, height, stride)[:, :, :, :columns]
    head_out = head_out + head_bias[:, None, None, None]
    latent = (
        (head_out - latent_mean[:, None, None, None])
        * latent_scale[:, None, None, None]
        * inside[None, :, None, :]
    ).astype(jnp.bfloat16)
    patches = latent.reshape(latent_dim, frame_count, height // 2, 2, columns // 2, 2)
    features = patches.transpose(3, 5, 0, 1, 2, 4).reshape(4 * latent_dim, -1)
    token_count = features.shape[1]
    replicas = lax.axis_size("dp")
    shards = lax.axis_size("seq")
    destinations = replicas * shards
    capacity = max(2, 2 * token_count // destinations)
    destination = token_dest[0, :, 0]
    matches = (destination[:, None] == jnp.arange(destinations, dtype=jnp.int32)[None, :]).astype(
        jnp.int32
    )
    before = (jnp.cumsum(matches, axis=0) - matches) * matches
    ranking = jnp.sum(before, axis=1)
    slot_index = destination * capacity + ranking
    placement = (
        slot_index[:, None] == jnp.arange(destinations * capacity, dtype=jnp.int32)[None, :]
    ).astype(jnp.bfloat16)
    buffer = jnp.einsum(
        "ts,ft->sf", placement, features, preferred_element_type=jnp.float32
    ).astype(jnp.bfloat16)
    buffer = buffer.reshape(replicas, shards, capacity * 4 * latent_dim)
    received_slots = lax.all_to_all(
        lax.all_to_all(buffer, "dp", split_axis=0, concat_axis=0, tiled=True),
        "seq",
        split_axis=1,
        concat_axis=1,
        tiled=True,
    )
    return received_slots.reshape(1, 1, destinations, capacity * 4 * latent_dim)


def solution(mesh):
    in_specs = (
        P("dp", "seq", None, None, None, None),
        P("dp", None),
        P("dp", None),
        P("dp", "seq", None),
        P(),
        P(),
        P(),
        P(),
        P(),
        P(),
        P(),
    )
    out_specs = P("dp", "seq", None, None)
    return jax.shard_map(
        on_device, mesh=mesh, in_specs=in_specs, out_specs=out_specs, check_vma=False
    )
```

profile of v0, /device:TPU:1, one launch (start us, length us, event | category | flops | bytes accessed | tf_op | source)
XLA Modules:
  0.0 110.9 jit_solution(212821886816148567)
XLA Ops:
  0.0 1.9 %slice_bitcast_fusion.1 = bf16[16,32,384]{2,1,0:T(8,128)(2,1)} fusion(bf16[4,2,16,32,384]{4,3,2,1,0:T(8,128)(2,1)} %bitcast.64), kind=kLoop, calls=%fused_computation.52 | loop fusion | bytes 786432 | tf_op jit(solution)/shard_map/squeeze | solution.py:95
  1.9 4.5 %collective-permute-start = (bf16[16,32,384]{2,1,0:T(8,128)(2,1)}, bf16[16,32,384]{2,1,0:T(8,128)(2,1)}, u32[]{:S(2)}, u32[]{:S(2)}) collective-permute-start(bf16[16,32,384]{2,1,0:T(8,128)(2,1)} %slice_bitcast_fusion.1), channel_id=1, source_target_pairs={{0,1},{1,2},{2,3},{3,4},{4,5},{5,6},{6,7},{7,8},{8,9},{9,10},{10,1... | collective-permute-start | bytes 1179656 | tf_op jit(solution)/shard_map/ppermute | solution.py:10
  6.4 2.4 %slice_bitcast_fusion = bf16[3,16,32,384]{3,2,1,0:T(8,128)(2,1)} fusion(bf16[4,2,16,32,384]{4,3,2,1,0:T(8,128)(2,1)} %bitcast.65), kind=kLoop, calls=%fused_computation.30 | loop fusion | bytes 2359296 | tf_op jit(solution)/shard_map/squeeze | solution.py:96
  8.9 2.1 %fusion.45 = (bf16[4,1,16,32,384]{4,3,2,1,0:T(8,128)(2,1)}, bf16[4,1,16,32,384]{4,3,2,1,0:T(8,128)(2,1)}) fusion(bf16[4,2,16,32,384]{4,3,2,1,0:T(8,128)(2,1)S(1)} %bitcast.66), kind=kLoop, calls=%fused_computation.101 | loop fusion | bytes 6291456 | tf_op jit(solution)/shard_map/slice | solution.py:33
  11.5 0.5 compare_convert_fusion.2
  12.0 0.5 compare_select_fusion
  13.0 2.9 %fusion.33 = f32[2048,384]{1,0:T(8,128)S(1)} fusion(bf16[2048,384]{1,0:T(8,128)(2,1)} %bitcast.70, bf16[3,384,384]{2,1,0:T(8,128)(2,1)} %param.15), kind=kOutput, calls=%fused_computation.53 | convolution fusion | flops 603979776 | bytes 5013504 | tf_op jit(solution)/shard_map/dot_general | solution.py:37
  16.0 1.1 %fusion.35 = f32[2048,384]{1,0:T(8,128)S(1)} fusion(bf16[2048,384]{1,0:T(8,128)(2,1)S(1)} %bitcast.69, bf16[3,384,384]{2,1,0:T(8,128)(2,1)S(1)} %copy-done.5), kind=kOutput, calls=%fused_computation.55 | convolution fusion | flops 603979776 | bytes 5013504 | tf_op jit(solution)/shard_map/dot_general | solution.py:32
  17.3 1.2 %pad_maximum_fusion = bf16[4,16,32,384]{3,2,1,0:T(8,128)(2,1)S(1)} fusion(bf16[3,16,32,384]{3,2,1,0:T(8,128)(2,1)S(1)} %copy-done.3, bf16[1,16,32,384]{3,2,1,0:T(8,128)(2,1)} %bitcast.10), kind=kLoop, calls=%fused_computation.29 | loop fusion | flops 786432 | bytes 3145728 | tf_op jit(solution)/shard_map/concatenate | solution.py:96
  18.5 1.1 %add_add_fusion = f32[2048,384]{1,0:T(8,128)S(1)} fusion(f32[2048,384]{1,0:T(8,128)S(1)} %fusion.33, f32[2048,384]{1,0:T(8,128)S(1)} %fusion.35, bf16[2048,384]{1,0:T(8,128)(2,1)S(1)} %bitcast.71, bf16[3,384,384]{2,1,0:T(8,128)(2,1)S(1)} %copy-done.5), kind=kOutput, calls=%fused_computation.26 | convolution fusion | flops 605552640 | bytes 11304960 | tf_op jit(solution)/shard_map/dot_general | solution.py:29
  19.7 0.7 fusion.8
  20.4 1.2 %fusion.16 = bf16[4,16,32,384]{3,2,1,0:T(8,128)(2,1)S(1)} fusion(bf16[4,16,32,384]{3,2,1,0:T(8,128)(2,1)S(1)} %get-tuple-element.8, f32[4,32]{1,0:T(4,128)S(1)} %fusion.41, f32[384]{0:T(512)S(1)} %copy-done.8, f32[4,16,32]{2,1,0:T(8,128)S(1)} %add_rsqrt_fusion), kind=kLoop, calls=%fused_computation.23 | loop fusion | flops 7077888 | bytes 3155968 | tf_op jit(solution)/shard_map/convert_element_type | solution.py:55
  21.7 2.1 %collective-permute-start.1 = (bf16[2,16,32,384]{3,2,1,0:T(8,128)(2,1)S(1)}, bf16[2,16,32,384]{3,2,1,0:T(8,128)(2,1)S(1)}, u32[]{:S(2)}, u32[]{:S(2)}) collective-permute-start(bf16[2,16,32,384]{3,2,1,0:T(8,128)(2,1)S(1)} %slice.189), channel_id=1, source_target_pairs={{0,1},{1,2},{2,3},{3,4},{4,5},{5,6},{6,7},{7,8},{8,9},{9,10},{10,1... | collective-permute-start | bytes 2359304 | tf_op jit(solution)/shard_map/ppermute | solution.py:10
  23.9 1.4 %broadcast_add_fusion = s32[512,8,64]{0,1,2:T(8,128)S(1)} fusion(s32[512,8,64]{0,1,2:T(8,128)} %bitcast.72, s32[512,8]{0,1:T(8,128)S(1)} %bitcast.75), kind=kLoop, calls=%fused_computation.50 | loop fusion | flops 262144 | bytes 2113536 | tf_op jit(solution)/shard_map/reduce_window_sum
  25.6 0.4 fusion.21
  26.0 6.6 %collective-permute-done.1 = bf16[2,16,32,384]{3,2,1,0:T(8,128)(2,1)S(1)} collective-permute-done((bf16[2,16,32,384]{3,2,1,0:T(8,128)(2,1)S(1)}, bf16[2,16,32,384]{3,2,1,0:T(8,128)(2,1)S(1)}, u32[]{:S(2)}, u32[]{:S(2)}) %collective-permute-start.1) | collective-permute-done | bytes 786464 | tf_op jit(solution)/shard_map/ppermute | solution.py:10
  32.5 3.3 %fusion.6 = bf16[6,19,34,384]{3,2,1,0:T(8,128)(2,1)} fusion(bf16[4,16,32,384]{3,2,1,0:T(8,128)(2,1)S(1)} %fusion.16, bf16[2,16,32,384]{3,2,1,0:T(8,128)(2,1)S(1)} %collective-permute-done.1), kind=kLoop, calls=%fused_computation.13 | loop fusion | flops 22325760 | bytes 5336064 | tf_op jit(solution)/shard_map/concatenate | solution.py:104
  35.8 3.9 %reshape.200 = bf16[3876,384]{1,0:T(8,128)(2,1)S(1)} reshape(bf16[6,19,34,384]{3,2,1,0:T(8,128)(2,1)} %fusion.6) | data formatting | bytes 5953536 | tf_op jit(solution)/shard_map/reshape | solution.py:108
  39.7 4.8 %convolution_bitcast_fusion = f32[432,3876]{1,0:T(8,128)} fusion(bf16[3876,384]{1,0:T(8,128)(2,1)S(1)} %reshape.200, bf16[432,384]{1,0:T(8,128)(2,1)S(1)} %bitcast.63), kind=kOutput, calls=%fused_computation.7 | convolution fusion | flops 1285963776 | bytes 10006272 | tf_op jit(solution)/shard_map/dot_general | solution.py:106
  44.5 11.1 %reshape.202 = f32[27,16,6,646]{3,2,1,0:T(8,128)} reshape(f32[432,3876]{1,0:T(8,128)} %convolution_bitcast_fusion) | data formatting | bytes 13395456 | tf_op jit(solution)/shard_map/reshape | solution.py:112
  55.7 4.6 %slice_add_fusion.16 = (f32[1,16,4,544]{3,2,1,0:T(4,128)S(1)}, f32[1,16,4,544]{3,2,1,0:T(4,128)S(1)}) fusion(f32[27,16,6,646]{3,2,1,0:T(8,128)} %reshape.202), kind=kLoop, calls=%fused_computation.77 | loop fusion | flops 557056 | bytes 2785280 | tf_op jit(solution)/shard_map/add | solution.py:65
  60.3 2.9 %slice_add_fusion.8 = f32[1,16,4,544]{3,2,1,0:T(4,128)S(1)} fusion(f32[27,16,6,646]{3,2,1,0:T(8,128)} %reshape.202), kind=kLoop, calls=%fused_computation.69 | loop fusion | flops 278528 | bytes 1392640 | tf_op jit(solution)/shard_map/add | solution.py:65
  63.1 0.4 reshape.217
  63.5 0.4 reshape.219
  63.9 0.4 reshape.218
  64.6 0.4 copy.54
  65.0 1.0 copy.55
  66.1 0.8 reshape.204
  66.8 0.5 fusion.19
  67.7 17.8 %all_to_all.10 = bf16[8,64,128]{2,1,0:T(8,128)(2,1)S(1)} all-to-all(bf16[8,64,128]{2,1,0:T(8,128)(2,1)S(1)} %reshape.205), channel_id=1, replica_groups=mesh['dp'=8,'seq'=64] {'dp'}, dimensions={0} | all-to-all | bytes 262144 | tf_op jit(solution)/shard_map/all_to_all | solution.py:149
  85.5 24.7 %all_to_all.11 = bf16[8,64,128]{2,0,1:T(8,128)(2,1)S(1)} all-to-all(bf16[8,64,128]{2,0,1:T(8,128)(2,1)S(1)} %copy.57), channel_id=1, replica_groups=mesh['dp'=8,'seq'=64] {'seq'}, dimensions={1} | all-to-all | bytes 262144 | tf_op jit(solution)/shard_map/all_to_all | solution.py:148
  110.2 0.7 copy.58
  (56 shorter events, 2.3 us)
Async XLA Ops:
  0.0 39.7 %copy-start = (bf16[3,3,3,384,16]{3,4,2,1,0:T(8,128)(2,1)S(1)}, bf16[3,3,3,384,16]{3,4,2,1,0:T(8,128)(2,1)}, u32[]{:S(2)}) copy-start(bf16[3,3,3,384,16]{3,4,2,1,0:T(8,128)(2,1)} %param.18) | copy-start | bytes 995332
  0.0 8.9 %copy-start.1 = (bf16[1,4,2,16,32,384]{5,4,3,2,1,0:T(8,128)(2,1)S(1)}, bf16[1,4,2,16,32,384]{5,4,3,2,1,0:T(8,128)(2,1)}, u32[]{:S(2)}) copy-start(bf16[1,4,2,16,32,384]{5,4,3,2,1,0:T(8,128)(2,1)} %param.11) | copy-start | bytes 9437188
  1.9 15.2 %collective-permute-start = (bf16[16,32,384]{2,1,0:T(8,128)(2,1)}, bf16[16,32,384]{2,1,0:T(8,128)(2,1)}, u32[]{:S(2)}, u32[]{:S(2)}) collective-permute-start(bf16[16,32,384]{2,1,0:T(8,128)(2,1)} %slice_bitcast_fusion.1), channel_id=1, source_target_pairs={{0,1},{1,2},{2,3},{3,4},{4,5},{5,6},{6,7},{7,8},{8,9},{9,10},{10,1... | collective-permute-start | bytes 1179656 | tf_op jit(solution)/shard_map/ppermute | solution.py:10
  8.9 2.1 %copy-start.14 = (s32[1,32]{1,0:T(1,128)S(1)}, s32[1,32]{1,0:T(1,128)}, u32[]{:S(2)}) copy-start(s32[1,32]{1,0:T(1,128)} %param.12) | copy-start | bytes 388
  8.9 2.4 %copy-start.16 = (s32[1,32]{1,0:T(1,128)S(1)}, s32[1,32]{1,0:T(1,128)}, u32[]{:S(2)}) copy-start(s32[1,32]{1,0:T(1,128)} %param.13) | copy-start | bytes 388
  8.9 3.6 %copy-start.6 = (s32[1,512,1]{1,2,0:T(1,128)S(1)}, s32[1,512,1]{1,2,0:T(1,128)}, u32[]{:S(2)}) copy-start(s32[1,512,1]{1,2,0:T(1,128)} %param.14) | copy-start | bytes 6148
  12.9 10.9 %copy-start.4 = (s32[512,4,128]{0,1,2:T(4,128)}, s32[512,4,128]{0,1,2:T(4,128)S(1)}, u32[]{:S(2)}) copy-start(s32[512,4,128]{0,1,2:T(4,128)S(1)} %fusion.23) | copy-start | bytes 3145732
  12.9 3.0 %copy-start.15 = (s32[4]{0:T(128)S(1)}, s32[4]{0:T(128)}, u32[]{:S(2)}) copy-start(s32[4]{0:T(128)} %compare_select_fusion) | copy-start | bytes 52
  12.9 3.1 %copy-start.2 = (bf16[4,1,16,32,384]{4,3,2,1,0:T(8,128)(2,1)S(1)}, bf16[4,1,16,32,384]{4,3,2,1,0:T(8,128)(2,1)}, u32[]{:S(2)}) copy-start(bf16[4,1,16,32,384]{4,3,2,1,0:T(8,128)(2,1)} %get-tuple-element.11) | copy-start | bytes 4718596
  13.0 3.1 %copy-start.5 = (bf16[3,384,384]{2,1,0:T(8,128)(2,1)S(1)}, bf16[3,384,384]{2,1,0:T(8,128)(2,1)}, u32[]{:S(2)}) copy-start(bf16[3,384,384]{2,1,0:T(8,128)(2,1)} %param.15) | copy-start | bytes 2654212
  16.0 1.3 %copy-start.3 = (bf16[3,16,32,384]{3,2,1,0:T(8,128)(2,1)S(1)}, bf16[3,16,32,384]{3,2,1,0:T(8,128)(2,1)}, u32[]{:S(2)}) copy-start(bf16[3,16,32,384]{3,2,1,0:T(8,128)(2,1)} %slice_bitcast_fusion) | copy-start | bytes 3538948
  18.5 1.2 %copy-start.7 = (f32[384]{0:T(512)S(1)}, f32[384]{0:T(512)}, u32[]{:S(2)}) copy-start(f32[384]{0:T(512)} %param.16) | copy-start | bytes 4612
  18.5 1.2 %copy-start.10 = (pred[4]{0:T(512)(128)(4,1)S(1)}, pred[4]{0:T(512)(128)(4,1)}, u32[]{:S(2)}) copy-start(pred[4]{0:T(512)(128)(4,1)} %get-tuple-element.16) | copy-start | bytes 16
  19.6 0.8 copy-start.8
  21.7 10.8 %collective-permute-start.1 = (bf16[2,16,32,384]{3,2,1,0:T(8,128)(2,1)S(1)}, bf16[2,16,32,384]{3,2,1,0:T(8,128)(2,1)S(1)}, u32[]{:S(2)}, u32[]{:S(2)}) collective-permute-start(bf16[2,16,32,384]{3,2,1,0:T(8,128)(2,1)S(1)} %slice.189), channel_id=1, source_target_pairs={{0,1},{1,2},{2,3},{3,4},{4,5},{5,6},{6,7},{7,8},{8,9},{9,10},{10,1... | collective-permute-start | bytes 2359304 | tf_op jit(solution)/shard_map/ppermute | solution.py:10
  55.7 8.6 %copy-start.9 = (f32[4]{0:T(128)S(1)}, f32[4]{0:T(128)}, u32[]{:S(2)}) copy-start(f32[4]{0:T(128)} %get-tuple-element.15) | copy-start | bytes 52
  55.7 8.7 %copy-start.11 = (f32[16]{0:T(128)S(1)}, f32[16]{0:T(128)}, u32[]{:S(2)}) copy-start(f32[16]{0:T(128)} %param.21) | copy-start | bytes 196
  55.7 8.7 %copy-start.12 = (f32[16]{0:T(128)S(1)}, f32[16]{0:T(128)}, u32[]{:S(2)}) copy-start(f32[16]{0:T(128)} %param.20) | copy-start | bytes 196
  55.7 8.7 %copy-start.13 = (f32[16]{0:T(128)S(1)}, f32[16]{0:T(128)}, u32[]{:S(2)}) copy-start(f32[16]{0:T(128)} %param.19) | copy-start | bytes 196
where the time goes:
time: 112 us; the launch traced here: 111 us
  blocking collectives  42.5 us (38%)
  local copies, waits for them, and re-layouts  26.8 us (24%)
  other arithmetic  17.6 us (16%)
  matrix products  10.6 us (9%)
  starting transfers between devices  6.6 us (6%)
  waiting for transfers between devices  6.57 us (6%)
    all_to_all x1, blocking collectives, on_device(): lax.all_to_all(lax.all_to_all(buffer, 'dp', split_axis=0, concat_axis=0,...  24.7 us
    all_to_all x1, blocking collectives, on_device(): lax.all_to_all(buffer, 'dp', split_axis=0, concat_axis=0, tiled=True)  17.8 us
    reshape x1, local copies, waits for them, and re-layouts, on_device(): products.reshape(27, latent_dim, frames_act.shape[0], (height + 3) * stride)  11.1 us
    add x2, other arithmetic, flat_taps(): running + products[(k * 3 + a) * 3 + b, :, :, offset:offset + span]  7.44 us
    ppermute x2, starting transfers between devices, from_behind(): lax.ppermute(value, axis, [(source, source + steps) for source in range(f...  6.6 us
    ppermute x2, waiting for transfers between devices, from_behind(): lax.ppermute(value, axis, [(source, source + steps) for source in range(f...  6.57 us
    dot_general x1, matrix products, on_device(): lax.dot_general(head_rows, padded.reshape(-1, channels), (((1,), (1,)), (...  4.82 us
    reshape x1, local copies, waits for them, and re-layouts, on_device(): padded.reshape(-1, channels)  3.87 us
  transfers between devices with their start and end apart: 2, of which 1 were waited for; matrix products, arithmetic and copies ran while one was open for 11% of the time, Pallas kernels for 0%

commit v1 on v0

--- a/solution.py
+++ b/solution.py
@@ -1,7 +1,124 @@
+import functools
+
 import jax
 import jax.numpy as jnp
 from jax import lax
+from jax.experimental import pallas as pl
+from jax.experimental.pallas import tpu as pltpu
 from jax.sharding import PartitionSpec as P
+
+CORES = 2
+
+
+def reorder(rows, source_of):
+    target = lax.broadcasted_iota(jnp.int32, (rows, rows), 0)
+    source = lax.broadcasted_iota(jnp.int32, (rows, rows), 1)
+    return jnp.where(source == source_of(target), 1.0, 0.0).astype(jnp.bfloat16)
+
+
+def moved(matrix, rows):
+    return jnp.dot(matrix, rows, preferred_element_type=jnp.float32).astype(jnp.bfloat16)
+
+
+def exchange_kernel(replicas, places, rows_ref, out_ref, first, middle, last, send_sem, recv_sem):
+    near = replicas * CORES
+    total = near * places
+    replica = lax.axis_index("dp")
+    shard = lax.axis_index("seq")
+    place = lax.div(shard, CORES)
+    core = lax.rem(shard, CORES)
+    mine = replica * CORES + core
+
+    def near_device(step):
+        index = lax.rem(mine + step, near)
+        return index, (lax.div(index, CORES), place * CORES + lax.rem(index, CORES))
+
+    def far_device(step):
+        index = lax.rem(place + step, places)
+        return index, (replica, index * CORES + core)
+
+    barrier = pltpu.get_barrier_semaphore()
+
+    def greet(find):
+        def body(step, carry):
+            pl.semaphore_signal(
+                barrier, inc=1, device_id=find(step)[1], device_id_type=pl.DeviceIdType.MESH
+            )
+            return carry
+        return body
+
+    lax.fori_loop(1, near, greet(near_device), 0)
+    lax.fori_loop(1, places, greet(far_device), 0)
+    pl.semaphore_wait(barrier, near - 1 + places - 1)
+
+    def near_send(step, carry):
+        index, device = near_device(step)
+        pltpu.make_async_remote_copy(
+            src_ref=rows_ref.at[pl.ds(index * places, places)],
+            dst_ref=first.at[pl.ds(mine * places, places)],
+            send_sem=send_sem.at[0],
+            recv_sem=recv_sem.at[0],
+            device_id=device,
+            device_id_type=pl.DeviceIdType.MESH,
+        ).start()
+        return carry
+
+    lax.fori_loop(1, near, near_send, 0)
+    own = pl.ds(mine * places, places)
+    first[own, :] = rows_ref[own, :]
+    turn = reorder(total, lambda row: lax.rem(row, near) * places + lax.div(row, near))
+    arrived = first.at[pl.ds(0, (near - 1) * places)]
+    pltpu.make_async_copy(arrived, arrived, recv_sem.at[0]).wait()
+    middle[...] = moved(turn, first[...])
+
+    def far_send(step, carry):
+        index, device = far_device(step)
+        pltpu.make_async_remote_copy(
+            src_ref=middle.at[pl.ds(index * near, near)],
+            dst_ref=last.at[pl.ds(place * near, near)],
+            send_sem=send_sem.at[1],
+            recv_sem=recv_sem.at[1],
+            device_id=device,
+            device_id_type=pl.DeviceIdType.MESH,
+        ).start()
+        return carry
+
+    lax.fori_loop(1, places, far_send, 0)
+    own = pl.ds(place * near, near)
+    last[own, :] = middle[own, :]
+
+    def slot(row):
+        source_replica = lax.div(row, places * CORES)
+        rest = lax.rem(row, places * CORES)
+        return lax.div(rest, CORES) * near + source_replica * CORES + lax.rem(rest, CORES)
+
+    back = reorder(total, slot)
+    arrived = last.at[pl.ds(0, (places - 1) * near)]
+    pltpu.make_async_copy(arrived, arrived, recv_sem.at[1]).wait()
+    out_ref[...] = moved(back, last[...])
+    sent = rows_ref.at[pl.ds(0, (near - 1) * places)]
+    pltpu.make_async_copy(sent, sent, send_sem.at[0]).wait()
+    sent = middle.at[pl.ds(0, (places - 1) * near)]
+    pltpu.make_async_copy(sent, sent, send_sem.at[1]).wait()
+
+
+def exchange(rows, replicas, shards):
+    total, width = rows.shape
+    places = shards // CORES
+    return pl.pallas_call(
+        functools.partial(exchange_kernel, replicas, places),
+        out_shape=jax.ShapeDtypeStruct((total, width), jnp.bfloat16),
+        in_specs=[pl.BlockSpec(memory_space=pltpu.VMEM)],
+        out_specs=pl.BlockSpec(memory_space=pltpu.VMEM),
+        scratch_shapes=[
+            pltpu.VMEM((total, width), jnp.bfloat16),
+            pltpu.VMEM((total, width), jnp.bfloat16),
+            pltpu.VMEM((total, width), jnp.bfloat16),
+            pltpu.SemaphoreType.DMA((2,)),
+            pltpu.SemaphoreType.DMA((2,)),
+        ],
+        compiler_params=pltpu.CompilerParams(collective_id=0, has_side_effects=True),
+    )(rows)
 
 
 def from_behind(value, axis, steps):
@@ -137,21 +254,20 @@
     )
     before = (jnp.cumsum(matches, axis=0) - matches) * matches
     ranking = jnp.sum(before, axis=1)
-    slot_index = destination * capacity + ranking
+    places = shards // CORES
+    ordered = (
+        (destination // shards * CORES + destination % CORES) * places
+        + destination % shards // CORES
+    )
+    slot_index = ordered * capacity + ranking
     placement = (
         slot_index[:, None] == jnp.arange(destinations * capacity, dtype=jnp.int32)[None, :]
     ).astype(jnp.bfloat16)
     buffer = jnp.einsum(
         "ts,ft->sf", placement, features, preferred_element_type=jnp.float32
     ).astype(jnp.bfloat16)
-    buffer = buffer.reshape(replicas, shards, capacity * 4 * latent_dim)
-    received_slots = lax.all_to_all(
-        lax.all_to_all(buffer, "dp", split_axis=0, concat_axis=0, tiled=True),
-        "seq",
-        split_axis=1,
-        concat_axis=1,
-        tiled=True,
-    )
+    buffer = buffer.reshape(destinations, capacity * 4 * latent_dim)
+    received_slots = exchange(buffer, replicas, shards)
     return received_slots.reshape(1, 1, destinations, capacity * 4 * latent_dim)
 
 

time: 112 us -> 102 us (0.911)
  blocking collectives: 42.5 us -> 0 us
  Pallas kernels: 0 us -> 31.2 us
  local copies, waits for them, and re-layouts: 26.8 us -> 28.2 us
    all_to_all x2 -> x0, blocking collectives: 42.5 us -> none  [the longest x1 24.7 us: on_device(): lax.all_to_all(lax.all_to_all(buffer, 'dp', split_axis=0, concat_axis=0,...]
    pallas_call x0 -> x1, Pallas kernels: none -> 31.2 us  [exchange(): pl.pallas_call(functools.partial(exchange_kernel, replicas, places), out_...]
    unnamed x35 -> x36, local copies, waits for them, and re-layouts: 0.2 us -> 1.77 us
  transfers between devices with their start and end apart: 2 -> 2, of which waited for: 1 -> 1; matrix products, arithmetic and copies ran while one was open for 11% -> 13% of each run, Pallas kernels for 0% -> 0%
where the time goes in v1:
time: 102 us; the launch traced here: 101 us
  Pallas kernels  31.2 us (31%)
  local copies, waits for them, and re-layouts  28.2 us (28%)
  other arithmetic  17.6 us (17%)
  matrix products  10.6 us (10%)
  starting transfers between devices  6.6 us (6%)
  waiting for transfers between devices  6.55 us (6%)
    pallas_call x1, Pallas kernels, exchange(): pl.pallas_call(functools.partial(exchange_kernel, replicas, places), out_...  31.2 us
    reshape x1, local copies, waits for them, and re-layouts, on_device(): products.reshape(27, latent_dim, frames_act.shape[0], (height + 3) * stride)  11.1 us
    add x2, other arithmetic, flat_taps(): running + products[(k * 3 + a) * 3 + b, :, :, offset:offset + span]  7.44 us
    ppermute x2, starting transfers between devices, from_behind(): lax.ppermute(value, axis, [(source, source + steps) for source in range(f...  6.6 us
    ppermute x2, waiting for transfers between devices, from_behind(): lax.ppermute(value, axis, [(source, source + steps) for source in range(f...  6.55 us
    dot_general x1, matrix products, on_device(): lax.dot_general(head_rows, padded.reshape(-1, channels), (((1,), (1,)), (...  4.82 us
    reshape x1, local copies, waits for them, and re-layouts, on_device(): padded.reshape(-1, channels)  3.87 us
    concatenate x1, other arithmetic, on_device(): frames_act = jnp.concatenate([received, activation], axis=0)  3.28 us
  transfers between devices with their start and end apart: 2, of which 1 were waited for; matrix products, arithmetic and copies ran while one was open for 13% of the time, Pallas kernels for 0%

profile of v1, /device:TPU:1, one launch (start us, length us, event | category | flops | bytes accessed | tf_op | source)
XLA Modules:
  0.0 101.1 jit_solution(8142429584953707289)
XLA Ops:
  0.0 1.9 %slice_bitcast_fusion.1 = bf16[16,32,384]{2,1,0:T(8,128)(2,1)} fusion(bf16[4,2,16,32,384]{4,3,2,1,0:T(8,128)(2,1)} %bitcast.64), kind=kLoop, calls=%fused_computation.52 | loop fusion | bytes 786432 | tf_op jit(solution)/shard_map/squeeze | solution.py:212
  1.9 4.5 %collective-permute-start = (bf16[16,32,384]{2,1,0:T(8,128)(2,1)}, bf16[16,32,384]{2,1,0:T(8,128)(2,1)}, u32[]{:S(2)}, u32[]{:S(2)}) collective-permute-start(bf16[16,32,384]{2,1,0:T(8,128)(2,1)} %slice_bitcast_fusion.1), channel_id=1, source_target_pairs={{0,1},{1,2},{2,3},{3,4},{4,5},{5,6},{6,7},{7,8},{8,9},{9,10},{10,1... | collective-permute-start | bytes 1179656 | tf_op jit(solution)/shard_map/ppermute | solution.py:127
  6.4 2.4 %slice_bitcast_fusion = bf16[3,16,32,384]{3,2,1,0:T(8,128)(2,1)} fusion(bf16[4,2,16,32,384]{4,3,2,1,0:T(8,128)(2,1)} %bitcast.65), kind=kLoop, calls=%fused_computation.30 | loop fusion | bytes 2359296 | tf_op jit(solution)/shard_map/squeeze | solution.py:213
  8.9 2.1 %fusion.55 = (bf16[4,1,16,32,384]{4,3,2,1,0:T(8,128)(2,1)}, bf16[4,1,16,32,384]{4,3,2,1,0:T(8,128)(2,1)}) fusion(bf16[4,2,16,32,384]{4,3,2,1,0:T(8,128)(2,1)S(1)} %bitcast.66), kind=kLoop, calls=%fused_computation.123 | loop fusion | bytes 6291456 | tf_op jit(solution)/shard_map/slice | solution.py:150
  11.5 0.5 compare_convert_fusion.2
  12.0 0.5 compare_select_fusion
  13.0 2.9 %fusion.33 = f32[2048,384]{1,0:T(8,128)S(1)} fusion(bf16[2048,384]{1,0:T(8,128)(2,1)} %bitcast.70, bf16[3,384,384]{2,1,0:T(8,128)(2,1)} %param.15), kind=kOutput, calls=%fused_computation.53 | convolution fusion | flops 603979776 | bytes 5013504 | tf_op jit(solution)/shard_map/dot_general | solution.py:154
  16.0 1.1 %fusion.35 = f32[2048,384]{1,0:T(8,128)S(1)} fusion(bf16[2048,384]{1,0:T(8,128)(2,1)S(1)} %bitcast.69, bf16[3,384,384]{2,1,0:T(8,128)(2,1)S(1)} %copy-done.5), kind=kOutput, calls=%fused_computation.55 | convolution fusion | flops 603979776 | bytes 5013504 | tf_op jit(solution)/shard_map/dot_general | solution.py:149
  17.3 1.2 %pad_maximum_fusion = bf16[4,16,32,384]{3,2,1,0:T(8,128)(2,1)S(1)} fusion(bf16[3,16,32,384]{3,2,1,0:T(8,128)(2,1)S(1)} %copy-done.3, bf16[1,16,32,384]{3,2,1,0:T(8,128)(2,1)} %bitcast.10), kind=kLoop, calls=%fused_computation.29 | loop fusion | flops 786432 | bytes 3145728 | tf_op jit(solution)/shard_map/concatenate | solution.py:213
  18.5 1.1 %add_add_fusion = f32[2048,384]{1,0:T(8,128)S(1)} fusion(f32[2048,384]{1,0:T(8,128)S(1)} %fusion.33, f32[2048,384]{1,0:T(8,128)S(1)} %fusion.35, bf16[2048,384]{1,0:T(8,128)(2,1)S(1)} %bitcast.71, bf16[3,384,384]{2,1,0:T(8,128)(2,1)S(1)} %copy-done.5), kind=kOutput, calls=%fused_computation.26 | convolution fusion | flops 605552640 | bytes 11304960 | tf_op jit(solution)/shard_map/dot_general | solution.py:146
  19.7 0.7 fusion.8
  20.4 1.2 %fusion.16 = bf16[4,16,32,384]{3,2,1,0:T(8,128)(2,1)S(1)} fusion(bf16[4,16,32,384]{3,2,1,0:T(8,128)(2,1)S(1)} %get-tuple-element.8, f32[4,32]{1,0:T(4,128)S(1)} %fusion.50, f32[384]{0:T(512)S(1)} %copy-done.8, f32[4,16,32]{2,1,0:T(8,128)S(1)} %add_rsqrt_fusion), kind=kLoop, calls=%fused_computation.23 | loop fusion | flops 7077888 | bytes 3155968 | tf_op jit(solution)/shard_map/convert_element_type | solution.py:172
  21.7 2.1 %collective-permute-start.1 = (bf16[2,16,32,384]{3,2,1,0:T(8,128)(2,1)S(1)}, bf16[2,16,32,384]{3,2,1,0:T(8,128)(2,1)S(1)}, u32[]{:S(2)}, u32[]{:S(2)}) collective-permute-start(bf16[2,16,32,384]{3,2,1,0:T(8,128)(2,1)S(1)} %slice.189), channel_id=1, source_target_pairs={{0,1},{1,2},{2,3},{3,4},{4,5},{5,6},{6,7},{7,8},{8,9},{9,10},{10,1... | collective-permute-start | bytes 2359304 | tf_op jit(solution)/shard_map/ppermute | solution.py:127
  23.9 1.4 %broadcast_add_fusion = s32[512,8,64]{0,1,2:T(8,128)S(1)} fusion(s32[512,8,64]{0,1,2:T(8,128)} %bitcast.72, s32[512,8]{0,1:T(8,128)S(1)} %bitcast.76), kind=kLoop, calls=%fused_computation.50 | loop fusion | flops 262144 | bytes 2113536 | tf_op jit(solution)/shard_map/reduce_window_sum
  25.6 0.4 fusion.21
  26.0 6.6 %collective-permute-done.1 = bf16[2,16,32,384]{3,2,1,0:T(8,128)(2,1)S(1)} collective-permute-done((bf16[2,16,32,384]{3,2,1,0:T(8,128)(2,1)S(1)}, bf16[2,16,32,384]{3,2,1,0:T(8,128)(2,1)S(1)}, u32[]{:S(2)}, u32[]{:S(2)}) %collective-permute-start.1) | collective-permute-done | bytes 786464 | tf_op jit(solution)/shard_map/ppermute | solution.py:127
  32.5 3.3 %fusion.6 = bf16[6,19,34,384]{3,2,1,0:T(8,128)(2,1)} fusion(bf16[4,16,32,384]{3,2,1,0:T(8,128)(2,1)S(1)} %fusion.16, bf16[2,16,32,384]{3,2,1,0:T(8,128)(2,1)S(1)} %collective-permute-done.1), kind=kLoop, calls=%fused_computation.13 | loop fusion | flops 22325760 | bytes 5336064 | tf_op jit(solution)/shard_map/concatenate | solution.py:221
  35.8 3.9 %reshape.283 = bf16[3876,384]{1,0:T(8,128)(2,1)S(1)} reshape(bf16[6,19,34,384]{3,2,1,0:T(8,128)(2,1)} %fusion.6) | data formatting | bytes 5953536 | tf_op jit(solution)/shard_map/reshape | solution.py:225
  39.7 4.8 %convolution_bitcast_fusion = f32[432,3876]{1,0:T(8,128)} fusion(bf16[3876,384]{1,0:T(8,128)(2,1)S(1)} %reshape.283, bf16[432,384]{1,0:T(8,128)(2,1)S(1)} %bitcast.63), kind=kOutput, calls=%fused_computation.7 | convolution fusion | flops 1285963776 | bytes 10006272 | tf_op jit(solution)/shard_map/dot_general | solution.py:223
  44.5 11.1 %reshape.285 = f32[27,16,6,646]{3,2,1,0:T(8,128)} reshape(f32[432,3876]{1,0:T(8,128)} %convolution_bitcast_fusion) | data formatting | bytes 13395456 | tf_op jit(solution)/shard_map/reshape | solution.py:229
  55.7 4.6 %slice_add_fusion.16 = (f32[1,16,4,544]{3,2,1,0:T(4,128)S(1)}, f32[1,16,4,544]{3,2,1,0:T(4,128)S(1)}) fusion(f32[27,16,6,646]{3,2,1,0:T(8,128)} %reshape.285), kind=kLoop, calls=%fused_computation.77 | loop fusion | flops 557056 | bytes 2785280 | tf_op jit(solution)/shard_map/add | solution.py:182
  60.3 2.9 %slice_add_fusion.8 = f32[1,16,4,544]{3,2,1,0:T(4,128)S(1)} fusion(f32[27,16,6,646]{3,2,1,0:T(8,128)} %reshape.285), kind=kLoop, calls=%fused_computation.69 | loop fusion | flops 278528 | bytes 1392640 | tf_op jit(solution)/shard_map/add | solution.py:182
  63.1 0.4 reshape.300
  63.5 0.4 reshape.302
  63.9 0.4 reshape.301
  64.6 0.4 copy.34
  65.0 1.0 %copy.35 = bf16[2,2,16,4,8,16]{5,4,3,2,1,0:T(8,128)(2,1)S(1)} copy(bf16[2,2,16,4,8,16]{2,1,5,0,4,3:T(2,128)(2,1)S(1)} %bitcast.74) | data formatting | bytes 131072 | tf_op jit(solution)/shard_map/transpose | solution.py:245
  66.1 0.8 reshape.287
  66.8 0.5 fusion.19
  67.5 0.8 reshape.288.rows_ref
  68.3 31.2 %shard_map.109 = bf16[512,128]{1,0:T(8,128)(2,1)} custom-call(bf16[512,128]{1,0:T(8,128)(2,1)} %reshape.288.rows_ref), custom_call_target="tpu_custom_call" | custom-call | tf_op jit(solution)/shard_map/pallas_call | solution.py:108
  99.5 1.6 %copy.38 = bf16[1,1,512,128]{3,2,1,0:T(8,128)(2,1)} copy(bf16[1,1,512,128]{3,2,1,0:T(8,128)(2,1)} %bitcast.75) | data formatting | bytes 262144
  (54 shorter events, 2.1 us)
Async XLA Ops:
  0.0 39.7 %copy-start = (bf16[3,3,3,384,16]{3,4,2,1,0:T(8,128)(2,1)S(1)}, bf16[3,3,3,384,16]{3,4,2,1,0:T(8,128)(2,1)}, u32[]{:S(2)}) copy-start(bf16[3,3,3,384,16]{3,4,2,1,0:T(8,128)(2,1)} %param.18) | copy-start | bytes 995332
  0.0 8.9 %copy-start.1 = (bf16[1,4,2,16,32,384]{5,4,3,2,1,0:T(8,128)(2,1)S(1)}, bf16[1,4,2,16,32,384]{5,4,3,2,1,0:T(8,128)(2,1)}, u32[]{:S(2)}) copy-start(bf16[1,4,2,16,32,384]{5,4,3,2,1,0:T(8,128)(2,1)} %param.11) | copy-start | bytes 9437188
  1.9 15.2 %collective-permute-start = (bf16[16,32,384]{2,1,0:T(8,128)(2,1)}, bf16[16,32,384]{2,1,0:T(8,128)(2,1)}, u32[]{:S(2)}, u32[]{:S(2)}) collective-permute-start(bf16[16,32,384]{2,1,0:T(8,128)(2,1)} %slice_bitcast_fusion.1), channel_id=1, source_target_pairs={{0,1},{1,2},{2,3},{3,4},{4,5},{5,6},{6,7},{7,8},{8,9},{9,10},{10,1... | collective-permute-start | bytes 1179656 | tf_op jit(solution)/shard_map/ppermute | solution.py:127
  8.9 2.1 %copy-start.14 = (s32[1,32]{1,0:T(1,128)S(1)}, s32[1,32]{1,0:T(1,128)}, u32[]{:S(2)}) copy-start(s32[1,32]{1,0:T(1,128)} %param.12) | copy-start | bytes 388
  8.9 2.4 %copy-start.16 = (s32[1,32]{1,0:T(1,128)S(1)}, s32[1,32]{1,0:T(1,128)}, u32[]{:S(2)}) copy-start(s32[1,32]{1,0:T(1,128)} %param.13) | copy-start | bytes 388
  8.9 3.6 %copy-start.6 = (s32[1,512,1]{1,2,0:T(1,128)S(1)}, s32[1,512,1]{1,2,0:T(1,128)}, u32[]{:S(2)}) copy-start(s32[1,512,1]{1,2,0:T(1,128)} %param.14) | copy-start | bytes 6148
  12.9 10.9 %copy-start.4 = (s32[512,4,128]{0,1,2:T(4,128)}, s32[512,4,128]{0,1,2:T(4,128)S(1)}, u32[]{:S(2)}) copy-start(s32[512,4,128]{0,1,2:T(4,128)S(1)} %fusion.23) | copy-start | bytes 3145732
  12.9 3.0 %copy-start.15 = (s32[4]{0:T(128)S(1)}, s32[4]{0:T(128)}, u32[]{:S(2)}) copy-start(s32[4]{0:T(128)} %compare_select_fusion) | copy-start | bytes 52
  12.9 3.1 %copy-start.2 = (bf16[4,1,16,32,384]{4,3,2,1,0:T(8,128)(2,1)S(1)}, bf16[4,1,16,32,384]{4,3,2,1,0:T(8,128)(2,1)}, u32[]{:S(2)}) copy-start(bf16[4,1,16,32,384]{4,3,2,1,0:T(8,128)(2,1)} %get-tuple-element.11) | copy-start | bytes 4718596
  13.0 3.1 %copy-start.5 = (bf16[3,384,384]{2,1,0:T(8,128)(2,1)S(1)}, bf16[3,384,384]{2,1,0:T(8,128)(2,1)}, u32[]{:S(2)}) copy-start(bf16[3,384,384]{2,1,0:T(8,128)(2,1)} %param.15) | copy-start | bytes 2654212
  16.0 1.3 %copy-start.3 = (bf16[3,16,32,384]{3,2,1,0:T(8,128)(2,1)S(1)}, bf16[3,16,32,384]{3,2,1,0:T(8,128)(2,1)}, u32[]{:S(2)}) copy-start(bf16[3,16,32,384]{3,2,1,0:T(8,128)(2,1)} %slice_bitcast_fusion) | copy-start | bytes 3538948
  18.5 1.2 %copy-start.7 = (f32[384]{0:T(512)S(1)}, f32[384]{0:T(512)}, u32[]{:S(2)}) copy-start(f32[384]{0:T(512)} %param.16) | copy-start | bytes 4612
  18.5 1.2 %copy-start.10 = (pred[4]{0:T(512)(128)(4,1)S(1)}, pred[4]{0:T(512)(128)(4,1)}, u32[]{:S(2)}) copy-start(pred[4]{0:T(512)(128)(4,1)} %get-tuple-element.16) | copy-start | bytes 16
  19.6 0.8 copy-start.8
  21.7 10.8 %collective-permute-start.1 = (bf16[2,16,32,384]{3,2,1,0:T(8,128)(2,1)S(1)}, bf16[2,16,32,384]{3,2,1,0:T(8,128)(2,1)S(1)}, u32[]{:S(2)}, u32[]{:S(2)}) collective-permute-start(bf16[2,16,32,384]{3,2,1,0:T(8,128)(2,1)S(1)} %slice.189), channel_id=1, source_target_pairs={{0,1},{1,2},{2,3},{3,4},{4,5},{5,6},{6,7},{7,8},{8,9},{9,10},{10,1... | collective-permute-start | bytes 2359304 | tf_op jit(solution)/shard_map/ppermute | solution.py:127
  55.7 8.6 %copy-start.9 = (f32[4]{0:T(128)S(1)}, f32[4]{0:T(128)}, u32[]{:S(2)}) copy-start(f32[4]{0:T(128)} %get-tuple-element.15) | copy-start | bytes 52
  55.7 8.7 %copy-start.11 = (f32[16]{0:T(128)S(1)}, f32[16]{0:T(128)}, u32[]{:S(2)}) copy-start(f32[16]{0:T(128)} %param.21) | copy-start | bytes 196
  55.7 8.7 %copy-start.12 = (f32[16]{0:T(128)S(1)}, f32[16]{0:T(128)}, u32[]{:S(2)}) copy-start(f32[16]{0:T(128)} %param.20) | copy-start | bytes 196
  55.7 8.7 %copy-start.13 = (f32[16]{0:T(128)S(1)}, f32[16]{0:T(128)}, u32[]{:S(2)}) copy-start(f32[16]{0:T(128)} %param.19) | copy-start | bytes 196

commit v2 on v0

v2 whole, which is shorter than its diff:
```python
import functools

import jax
import jax.numpy as jnp
from jax import lax
from jax.experimental import pallas as pl
from jax.experimental.pallas import tpu as pltpu
from jax.sharding import PartitionSpec as P

CORES = 2
ALONG_X = 4
CHUNKS = 4
MESH = pl.DeviceIdType.MESH
F32 = jnp.float32
BF16 = jnp.bfloat16


def iota(shape, axis):
    return lax.broadcasted_iota(jnp.int32, shape, axis)


def reorder(rows, source_of):
    source = source_of(iota((rows, 1), 0))
    return jnp.where(iota((rows, rows), 1) == source, 1.0, 0.0).astype(BF16)


def column_of(row):
    count = row.shape[1]
    diagonal = iota((count, count), 0) == iota((count, count), 1)
    return jnp.sum(jnp.where(diagonal, row, 0.0), axis=1, keepdims=True)


def frame_facts(lengths, resolutions, first_frame, total_frames, columns):
    clips = lengths.shape[1]
    earlier = iota((clips, clips), 1) < iota((clips, clips), 0)
    own = iota((clips, clips), 1) == iota((clips, clips), 0)
    starts = jnp.sum(jnp.where(earlier, lengths, 0.0), axis=1, keepdims=True)
    ends = starts + column_of(lengths)
    resolution = jnp.sum(jnp.where(own, resolutions, 0.0), axis=1, keepdims=True)
    frame = (first_frame + iota((clips, 128), 1)).astype(F32)
    belongs = (frame >= starts) & (frame < ends)
    start = jnp.sum(jnp.where(belongs, starts, 0.0), axis=0, keepdims=True)
    kind = jnp.sum(jnp.where(belongs, resolution, 0.0), axis=0, keepdims=True)
    frame = frame[:1]
    exists = frame < float(total_frames)
    first = jnp.where(frame == start, 1.0, 0.0)
    one = jnp.where((frame - 1.0 >= start) & exists, 1.0, 0.0)
    two = jnp.where((frame - 2.0 >= start) & exists, 1.0, 0.0)
    limit = jnp.where(kind == 1.0, float(columns), float(columns * 13 // 20))
    return first, one, two, limit


def pick(row, index):
    return jnp.sum(jnp.where(iota(row.shape, 1) == index, row, 0.0), axis=1, keepdims=True)


def spatial_sum(taps, latent_dim, columns):
    cells = taps.shape[1]
    band = 3 * latent_dim
    cell = iota((1, cells), 1)
    column = lax.rem(cell, columns)
    above = jnp.where(cell >= columns, pltpu.roll(taps[:band], columns, 1), 0.0)
    below = jnp.where(cell < cells - columns, pltpu.roll(taps[2 * band :], cells - columns, 1), 0.0)
    rows = taps[band : 2 * band] + above + below
    left = jnp.where(column >= 1, pltpu.roll(rows[:latent_dim], 1, 1), 0.0)
    right = jnp.where(column < columns - 1, pltpu.roll(rows[2 * latent_dim :], cells - 1, 1), 0.0)
    return rows[latent_dim : 2 * latent_dim] + left + right


def activated(section, passed, first, gain, limit, columns):
    rows, channels = section.shape
    section = jnp.where(first > 0.5, passed.astype(F32), section).astype(BF16).astype(F32)
    mean_square = jnp.sum(section * section, axis=1, keepdims=True) * (1.0 / channels)
    column = lax.rem(iota((rows, 1), 0), columns).astype(F32)
    inside = jnp.where(column < limit, 0.5, 0.0)
    half = section * (lax.rsqrt(mean_square + 1e-06) * 0.5) * gain
    return (half * 2.0 * (inside + inside * jnp.tanh(half))).astype(BF16)


def encode_kernel(
    replicas,
    places,
    height,
    columns,
    frames_hbm,
    clip_hbm,
    res_hbm,
    dest_hbm,
    tconv_hbm,
    bias_hbm,
    gain_hbm,
    head_hbm,
    head_bias_hbm,
    mean_hbm,
    scale_hbm,
    out_ref,
    frames,
    clip,
    res,
    dest,
    tconv,
    bias,
    gain,
    head,
    head_bias,
    mean,
    scale,
    carried,
    halo_in,
    halo_out,
    section,
    active,
    products,
    latents,
    match,
    turn,
    back,
    unpatch,
    outgoing,
    first_stage,
    middle,
    last_stage,
    load_sem,
    carry_send,
    carry_recv,
    halo_sem,
    ready_sem,
    send_sem,
    recv_sem,
):
    near = replicas * CORES
    total = near * places
    shards = places * CORES
    along_y = places // ALONG_X
    frame_count = frames.shape[0] // 2
    cells, channels = frames.shape[1:]
    latent_dim = head_bias.shape[1]
    taps = 9 * latent_dim
    replica = lax.axis_index("dp")
    shard = lax.axis_index("seq")
    place = lax.div(shard, CORES)
    core = lax.rem(shard, CORES)
    x = lax.rem(place, ALONG_X)
    y = lax.div(place, ALONG_X)
    mine = replica * CORES + core
    after = (replica, lax.rem(shard + 1, shards))
    before = (replica, lax.rem(shard + shards - 1, shards))

    def near_device(step):
        index = lax.rem(mine + step, near)
        return index, (lax.div(index, CORES), place * CORES + lax.rem(index, CORES))

    def far_device(step):
        index = lax.rem(place + step, places)
        return index, (replica, index * CORES + core)

    def z_device(step):
        return (lax.rem(replica + step, replicas), shard)

    def y_device(step):
        return (replica, (lax.rem(y + step, along_y) * ALONG_X + x) * CORES + core)

    def x_device(step):
        return (replica, (y * ALONG_X + lax.rem(x + step, ALONG_X)) * CORES + core)

    other_core = (replica, place * CORES + 1 - core)

    barrier = pltpu.get_barrier_semaphore()

    def signal(semaphore, device):
        pl.semaphore_signal(semaphore, inc=1, device_id=device, device_id_type=MESH)

    signal(barrier, before)
    signal(barrier, other_core)
    for step in range(1, ALONG_X):
        signal(barrier, x_device(step))
    for step in range(1, along_y):
        signal(barrier, y_device(step))
    for step in range(1, replicas):
        signal(barrier, z_device(step))

    loads = [
        (clip_hbm, clip),
        (res_hbm, res),
        (dest_hbm, dest),
        (bias_hbm, bias),
        (gain_hbm, gain),
        (head_bias_hbm, head_bias),
        (mean_hbm, mean),
        (scale_hbm, scale),
        (tconv_hbm, tconv),
        (head_hbm, head),
    ]
    for index in range(frame_count):
        pair = pl.ds(2 * index, 2)
        loads.append((frames_hbm.at[pair], frames.at[pair]))
    loads = [
        pltpu.make_async_copy(source, target, load_sem.at[index])
        for index, (source, target) in enumerate(loads)
    ]
    for load in loads:
        load.start()

    def patch_of(cell):
        row, column = lax.div(cell, columns), lax.rem(cell, columns)
        part = lax.rem(row, 2) * 2 + lax.rem(column, 2)
        return part * (cells // 4) + lax.div(row, 2) * (columns // 2) + lax.div(column, 2)

    def slot(row):
        rest = lax.rem(row, shards)
        return lax.div(rest, CORES) * near + lax.div(row, shards) * CORES + lax.rem(rest, CORES)

    unpatch[...] = reorder(cells, patch_of)
    turn[...] = reorder(total, lambda row: lax.rem(row, near) * places + lax.div(row, near))
    back[...] = reorder(total, slot)

    for load in loads[:8]:
        load.wait()
    first_frame = shard * frame_count
    first, one, two, limit = frame_facts(
        clip[...].astype(F32), res[...].astype(F32), first_frame, shards * frame_count, columns
    )
    row = iota((total, 1), 0)
    owner, spot = lax.div(row, places), lax.rem(row, places)
    named = lax.div(owner, CORES) * shards + spot * CORES + lax.rem(owner, CORES)
    tokens = dest.shape[1]
    matches = dest[...] == named
    match[...] = jnp.where(matches, 1.0, 0.0).astype(BF16)
    sooner = jnp.where(iota((tokens, tokens), 0) < iota((tokens, tokens), 1), 1.0, 0.0).astype(BF16)
    counts = jnp.dot(match[...], sooner, preferred_element_type=F32)
    rank = jnp.sum(jnp.where(matches, counts, 0.0), axis=0, keepdims=True)
    bias_row = bias[...].reshape(1, channels)
    gain_row = gain[...].reshape(1, channels)
    head_bias_column = column_of(head_bias[...])
    mean_column = column_of(mean[...])
    scale_column = column_of(scale[...])

    pl.semaphore_wait(barrier, 1 + 1 + ALONG_X - 1 + along_y - 1 + replicas - 1)
    rows = cells // CHUNKS
    sends = []
    for chunk in range(CHUNKS):
        part = pl.ds(chunk * rows, rows)
        sends.append(
            pltpu.make_async_remote_copy(
                src_ref=frames_hbm.at[2 * frame_count - 1, part],
                dst_ref=carried.at[part],
                send_sem=carry_send.at[chunk],
                recv_sem=carry_recv.at[chunk],
                device_id=after,
                device_id_type=MESH,
            )
        )
        sends[-1].start()
    signal(ready_sem, other_core)
    for step in range(1, ALONG_X):
        signal(ready_sem, x_device(step))

    for load in loads[8:]:
        load.wait()

    def section_frame(index, carry):
        taken = jnp.concatenate(
            [frames[2 * index - 1], frames[2 * index], frames[2 * index + 1]], axis=1
        )
        section[...] = jnp.dot(taken, tconv[...], preferred_element_type=F32)
        is_first, inside = pick(first, index), pick(limit, index)

        def part_of(chunk, carry):
            part = pl.ds(pl.multiple_of(chunk * rows, rows), rows)
            active[part, :] = activated(
                section[part, :] + bias_row,
                frames[2 * index + 1, part, :],
                is_first,
                gain_row,
                inside,
                columns,
            )
            return carry

        lax.fori_loop(0, CHUNKS, part_of, 0)
        products[index] = lax.dot_general(
            head[...], active[...], (((1,), (1,)), ((), ())), preferred_element_type=F32
        )
        return carry

    lax.fori_loop(1, frame_count, section_frame, 0)

    def tap_block(index, k):
        return products[index, k * taps : (k + 1) * taps]

    halo_out[0] = spatial_sum(
        tap_block(frame_count - 2, 0) * pick(two, frame_count)
        + tap_block(frame_count - 1, 1) * pick(one, frame_count),
        latent_dim,
        columns,
    )
    halo_out[1] = spatial_sum(
        tap_block(frame_count - 1, 0) * pick(two, frame_count + 1), latent_dim, columns
    )
    halo = pltpu.make_async_remote_copy(
        src_ref=halo_out,
        dst_ref=halo_in,
        send_sem=halo_sem.at[0],
        recv_sem=halo_sem.at[1],
        device_id=after,
        device_id_type=MESH,
    )
    halo.start()

    for index in range(1, frame_count):
        block = tap_block(index, 2)
        if index >= 2:
            block = block + tap_block(index - 1, 1) * pick(one, index)
        if index >= 3:
            block = block + tap_block(index - 2, 0) * pick(two, index)
        latents[index] = spatial_sum(block, latent_dim, columns)

    section[...] = jnp.dot(
        jnp.concatenate([frames[0], frames[1]], axis=1),
        tconv[channels:, :],
        preferred_element_type=F32,
    )
    is_first, inside = pick(first, 0), pick(limit, 0)
    for chunk in range(CHUNKS):
        part = pl.ds(chunk * rows, rows)
        sends[chunk].wait_recv()
        summed = section[part, :] + jnp.dot(
            carried[part, :], tconv[:channels, :], preferred_element_type=F32
        )
        act = activated(
            summed + bias_row, frames[1, part, :], is_first, gain_row, inside, columns
        )
        products[0, :, part] = lax.dot_general(
            head[...], act, (((1,), (1,)), ((), ())), preferred_element_type=F32
        )

    latents[0] = spatial_sum(tap_block(0, 2), latent_dim, columns)
    latents[1] += spatial_sum(tap_block(0, 1) * pick(one, 1), latent_dim, columns)
    latents[2] += spatial_sum(tap_block(0, 0) * pick(two, 2), latent_dim, columns)
    halo.wait_recv()
    latents[0] += halo_in[0]
    latents[1] += halo_in[1]
    column = lax.rem(iota((1, cells), 1), columns).astype(F32)
    finished = []
    for index in range(frame_count):
        inside = jnp.where(column < pick(limit, index), 1.0, 0.0)
        value = (latents[index] + head_bias_column - mean_column) * scale_column * inside
        finished.append(value.astype(BF16))
    parts = jnp.dot(
        jnp.concatenate(finished, axis=0), unpatch[...], preferred_element_type=F32
    )
    patch_count = cells // 4
    features = jnp.concatenate(
        [
            jnp.concatenate(
                [
                    parts[
                        index * latent_dim : (index + 1) * latent_dim,
                        quarter * patch_count : (quarter + 1) * patch_count,
                    ]
                    for index in range(frame_count)
                ],
                axis=1,
            )
            for quarter in range(4)
        ],
        axis=0,
    )
    ranked = jnp.concatenate(
        [jnp.where(rank == 0.0, features, 0.0), jnp.where(rank == 1.0, features, 0.0)], axis=0
    ).astype(BF16)
    outgoing[...] = lax.dot_general(
        match[...], ranked, (((1,), (1,)), ((), ())), preferred_element_type=F32
    ).astype(BF16)

    pl.semaphore_wait(ready_sem, 1 + ALONG_X - 1)

    def near_send(step, carry):
        index, device = near_device(step)
        pltpu.make_async_remote_copy(
            src_ref=outgoing.at[pl.ds(index * places, places)],
            dst_ref=first_stage.at[pl.ds(mine * places, places)],
            send_sem=send_sem.at[0],
            recv_sem=recv_sem.at[0],
            device_id=device,
            device_id_type=MESH,
        ).start()
        return carry

    lax.fori_loop(1, near, near_send, 0)
    own = pl.ds(mine * places, places)
    first_stage[own, :] = outgoing[own, :]
    arrived = first_stage.at[pl.ds(0, (near - 1) * places)]
    pltpu.make_async_copy(arrived, arrived, recv_sem.at[0]).wait()
    middle[...] = jnp.dot(turn[...], first_stage[...], preferred_element_type=F32).astype(BF16)

    def far_send(step, carry):
        index, device = far_device(step)
        pltpu.make_async_remote_copy(
            src_ref=middle.at[pl.ds(index * near, near)],
            dst_ref=last_stage.at[pl.ds(place * near, near)],
            send_sem=send_sem.at[1],
            recv_sem=recv_sem.at[1],
            device_id=device,
            device_id_type=MESH,
        ).start()
        return carry

    lax.fori_loop(1, places, far_send, 0)
    own = pl.ds(place * near, near)
    last_stage[own, :] = middle[own, :]
    for chunk in range(CHUNKS):
        sends[chunk].wait_send()
    halo.wait_send()
    sent = outgoing.at[pl.ds(0, (near - 1) * places)]
    pltpu.make_async_copy(sent, sent, send_sem.at[0]).wait()
    arrived = last_stage.at[pl.ds(0, (places - 1) * near)]
    pltpu.make_async_copy(arrived, arrived, recv_sem.at[1]).wait()
    out_ref[...] = jnp.dot(back[...], last_stage[...], preferred_element_type=F32)
    sent = middle.at[pl.ds(0, (places - 1) * near)]
    pltpu.make_async_copy(sent, sent, send_sem.at[1]).wait()


def on_device(
    replicas,
    shards,
    frames_in,
    clip_frames,
    res_ids,
    token_dest,
    tconv_weight,
    tconv_bias,
    head_gain,
    head_weight,
    head_bias,
    latent_mean,
    latent_scale,
):
    _, frame_count, slots, height, columns, channels = frames_in.shape
    latent_dim = head_weight.shape[-1]
    cells = height * columns
    tokens = token_dest.shape[1]
    clips = clip_frames.shape[1]
    destinations = replicas * shards
    width = 2 * 4 * latent_dim
    places = shards // CORES
    operands = (
        frames_in.reshape(frame_count * slots, cells, channels),
        clip_frames,
        res_ids,
        token_dest.reshape(1, tokens),
        tconv_weight.reshape(3 * channels, channels),
        tconv_bias,
        head_gain,
        jnp.transpose(head_weight, (0, 1, 2, 4, 3)).reshape(27 * latent_dim, channels),
        head_bias.reshape(1, latent_dim),
        latent_mean.reshape(1, latent_dim),
        latent_scale.reshape(1, latent_dim),
    )
    square = pltpu.VMEM((destinations, destinations), BF16)
    exchanged = pltpu.VMEM((destinations, width), BF16)
    slots_out = pl.pallas_call(
        functools.partial(encode_kernel, replicas, places, height, columns),
        out_shape=jax.ShapeDtypeStruct((destinations, width), F32),
        in_specs=[pl.BlockSpec(memory_space=pltpu.HBM)] * len(operands),
        out_specs=pl.BlockSpec(memory_space=pltpu.VMEM),
        scratch_shapes=[
            pltpu.VMEM(operand.shape, operand.dtype) for operand in operands
        ]
        + [
            pltpu.VMEM((cells, channels), BF16),
            pltpu.VMEM((2, latent_dim, cells), F32),
            pltpu.VMEM((2, latent_dim, cells), F32),
            pltpu.VMEM((cells, channels), F32),
            pltpu.VMEM((cells, channels), BF16),
            pltpu.VMEM((frame_count, 27 * latent_dim, cells), F32),
            pltpu.VMEM((frame_count, latent_dim, cells), F32),
            pltpu.VMEM((destinations, tokens), BF16),
            square,
            square,
            pltpu.VMEM((cells, cells), BF16),
            exchanged,
            exchanged,
            exchanged,
            exchanged,
            pltpu.SemaphoreType.DMA((10 + frame_count,)),
            pltpu.SemaphoreType.DMA((CHUNKS,)),
            pltpu.SemaphoreType.DMA((CHUNKS,)),
            pltpu.SemaphoreType.DMA((2,)),
            pltpu.SemaphoreType.REGULAR,
            pltpu.SemaphoreType.DMA((2,)),
            pltpu.SemaphoreType.DMA((2,)),
        ],
        compiler_params=pltpu.CompilerParams(
            collective_id=0, has_side_effects=True, vmem_limit_bytes=60 * 1024 * 1024
        ),
        name="encode_and_route",
    )(*operands)
    return slots_out.astype(BF16).reshape(1, 1, destinations, width)


def solution(mesh):
    in_specs = (
        P("dp", "seq", None, None, None, None),
        P("dp", None),
        P("dp", None),
        P("dp", "seq", None),
        P(),
        P(),
        P(),
        P(),
        P(),
        P(),
        P(),
    )
    out_specs = P("dp", "seq", None, None)
    return jax.shard_map(
        functools.partial(on_device, mesh.shape["dp"], mesh.shape["seq"]),
        mesh=mesh,
        in_specs=in_specs,
        out_specs=out_specs,
        check_vma=False,
    )
```

time: 112 us -> 42 us (0.38)
  blocking collectives: 42.5 us -> 0 us
  Pallas kernels: 0 us -> 40.2 us
  local copies, waits for them, and re-layouts: 26.8 us -> 0 us
  other arithmetic: 17.6 us -> 1.62 us
  matrix products: 10.6 us -> 0 us
  starting transfers between devices: 6.6 us -> 0 us
  waiting for transfers between devices: 6.57 us -> 0 us
    all_to_all x2 -> x0, blocking collectives: 42.5 us -> none  [the longest x1 24.7 us: on_device(): lax.all_to_all(lax.all_to_all(buffer, 'dp', split_axis=0, concat_axis=0,...]
    pallas_call x0 -> x1, Pallas kernels: none -> 40.2 us  [on_device(): pl.pallas_call(functools.partial(encode_kernel, replicas, places, height,...]
    reshape x4 -> x0, local copies, waits for them, and re-layouts: 15.9 us -> none  [the longest x1 11.1 us: on_device(): products.reshape(27, latent_dim, frames_act.shape[0], (height + 3) * stride)]
    dot_general x5 -> x0, matrix products: 10.6 us -> none  [the longest x1 4.82 us: on_device(): lax.dot_general(head_rows, padded.reshape(-1, channels), (((1,), (1,)), (...]
    add x4 -> x0, other arithmetic: 7.45 us -> none  [the longest x2 7.44 us: flat_taps(): running + products[(k * 3 + a) * 3 + b, :, :, offset:offset + span]]
    ppermute x2 -> x0, starting transfers between devices: 6.6 us -> none  [from_behind(): lax.ppermute(value, axis, [(source, source + steps) for source in range(f...]
    ppermute x2 -> x0, waiting for transfers between devices: 6.57 us -> none  [from_behind(): lax.ppermute(value, axis, [(source, source + steps) for source in range(f...]
    concatenate x2 -> x0, other arithmetic: 4.46 us -> none  [the longest x1 3.28 us: on_device(): frames_act = jnp.concatenate([received, activation], axis=0)]
  transfers between devices with their start and end apart: 2 -> 0, of which waited for: 1 -> 0; matrix products, arithmetic and copies ran while one was open for 11% -> 0% of each run, Pallas kernels for 0% -> 0%
where the time goes in v2:
time: 42 us; the launch traced here: 41.8 us
  Pallas kernels  40.2 us (96%)
  other arithmetic  1.62 us (4%)
    pallas_call x1, Pallas kernels, on_device(): pl.pallas_call(functools.partial(encode_kernel, replicas, places, height,...  40.2 us
    reshape x1, other arithmetic, on_device(): return slots_out.astype(BF16).reshape(1, 1, destinations, width)  1.62 us

profile of v2, /device:TPU:1, one launch (start us, length us, event | category | flops | bytes accessed | tf_op | source)
XLA Modules:
  0.0 41.8 jit_solution(8377249367248524581)
XLA Ops:
  0.0 40.2 %encode_and_route.1 = f32[512,128]{1,0:T(8,128)} custom-call(bf16[8,512,384]{2,1,0:T(8,128)(2,1)} %bitcast.11, s32[1,32]{1,0:T(1,128)} %clip_hbm.1, s32[1,32]{1,0:T(1,128)} %res_hbm.1, s32[1,512]{1,0:T(1,128)} %bitcast.14, bf16[1152,384]{1,0:T(8,128)(2,1)} %bitcast.12, f32[384]{0:T(512)} %bias_hbm.1, f32[384]{0:T(512)} %gain_hbm.1, ...), custom_call_target="tpu_custom_call" | custom-call | tf_op jit(solution)/shard_map/encode_and_route/pallas_call | solution.py:462
  40.2 1.6 %convert_bitcast_fusion = bf16[1,1,512,128]{3,2,1,0:T(8,128)(2,1)} fusion(f32[512,128]{1,0:T(8,128)} %encode_and_route.1), kind=kLoop, calls=%fused_computation | loop fusion | flops 65536 | bytes 393216 | tf_op jit(solution)/shard_map/reshape | solution.py:499

commit v3 on v2

--- a/solution.py
+++ b/solution.py
@@ -9,7 +9,7 @@
 
 CORES = 2
 ALONG_X = 4
-CHUNKS = 4
+CHUNKS = 2
 MESH = pl.DeviceIdType.MESH
 F32 = jnp.float32
 BF16 = jnp.bfloat16
@@ -155,51 +155,40 @@
         return index, (replica, index * CORES + core)
 
     def z_device(step):
-        return (lax.rem(replica + step, replicas), shard)
+        return (lax.rem(replica + step + replicas, replicas), shard)
 
     def y_device(step):
-        return (replica, (lax.rem(y + step, along_y) * ALONG_X + x) * CORES + core)
+        return (replica, (lax.rem(y + step + along_y, along_y) * ALONG_X + x) * CORES + core)
 
     def x_device(step):
-        return (replica, (y * ALONG_X + lax.rem(x + step, ALONG_X)) * CORES + core)
+        return (replica, (y * ALONG_X + lax.rem(x + step + ALONG_X, ALONG_X)) * CORES + core)
 
     other_core = (replica, place * CORES + 1 - core)
 
     barrier = pltpu.get_barrier_semaphore()
 
-    def signal(semaphore, device):
-        pl.semaphore_signal(semaphore, inc=1, device_id=device, device_id_type=MESH)
-
-    signal(barrier, before)
-    signal(barrier, other_core)
-    for step in range(1, ALONG_X):
-        signal(barrier, x_device(step))
-    for step in range(1, along_y):
-        signal(barrier, y_device(step))
-    for step in range(1, replicas):
-        signal(barrier, z_device(step))
-
-    loads = [
-        (clip_hbm, clip),
-        (res_hbm, res),
-        (dest_hbm, dest),
-        (bias_hbm, bias),
-        (gain_hbm, gain),
-        (head_bias_hbm, head_bias),
-        (mean_hbm, mean),
-        (scale_hbm, scale),
-        (tconv_hbm, tconv),
-        (head_hbm, head),
-    ]
-    for index in range(frame_count):
-        pair = pl.ds(2 * index, 2)
-        loads.append((frames_hbm.at[pair], frames.at[pair]))
+    def signal(semaphore, *devices):
+        for device in devices:
+            pl.semaphore_signal(semaphore, inc=1, device_id=device, device_id_type=MESH)
+
+    signal(barrier, before, other_core, x_device(1), x_device(-1))
+    signal(barrier, y_device(1), y_device(-1), z_device(1), z_device(-1))
+
+    wanted = [(tconv_hbm, tconv)]
+    wanted += [(frames_hbm.at[index], frames.at[index]) for index in (3, 4, 5, 6, 7)]
+    wanted += [(head_hbm, head), (bias_hbm, bias), (gain_hbm, gain), (clip_hbm, clip), (res_hbm, res)]
+    wanted += [(frames_hbm.at[index], frames.at[index]) for index in (2, 1, 0)]
+    wanted += [(dest_hbm, dest), (head_bias_hbm, head_bias), (mean_hbm, mean), (scale_hbm, scale)]
     loads = [
         pltpu.make_async_copy(source, target, load_sem.at[index])
-        for index, (source, target) in enumerate(loads)
+        for index, (source, target) in enumerate(wanted)
     ]
     for load in loads:
         load.start()
+
+    def arrive(first_load, last_load):
+        for load in loads[first_load : last_load + 1]:
+            load.wait()
 
     def patch_of(cell):
         row, column = lax.div(cell, columns), lax.rem(cell, columns)
@@ -214,12 +203,116 @@
     turn[...] = reorder(total, lambda row: lax.rem(row, near) * places + lax.div(row, near))
     back[...] = reorder(total, slot)
 
-    for load in loads[:8]:
-        load.wait()
+
+    rows = cells // CHUNKS
+    sends = [
+        pltpu.make_async_remote_copy(
+            src_ref=frames_hbm.at[2 * frame_count - 1, pl.ds(chunk * rows, rows)],
+            dst_ref=carried.at[pl.ds(chunk * rows, rows)],
+            send_sem=carry_send.at[chunk],
+            recv_sem=carry_recv.at[chunk],
+            device_id=after,
+            device_id_type=MESH,
+        )
+        for chunk in range(CHUNKS)
+    ]
+    pl.semaphore_wait(barrier, 8)
+    for send in sends:
+        send.start()
+    signal(ready_sem.at[0], x_device(1), y_device(1), y_device(-1), z_device(1), z_device(-1))
+
+    arrive(7, 10)
     first_frame = shard * frame_count
     first, one, two, limit = frame_facts(
         clip[...].astype(F32), res[...].astype(F32), first_frame, shards * frame_count, columns
     )
+    bias_row = bias[...].reshape(1, channels)
+    gain_row = gain[...].reshape(1, channels)
+
+    def part_of(chunk):
+        return slice(chunk * rows, (chunk + 1) * rows)
+
+    def section_of(index, chunk, spot):
+        part = part_of(chunk)
+        taken = jnp.concatenate(
+            [frames[2 * index - 1, part], frames[2 * index, part], frames[2 * index + 1, part]],
+            axis=1,
+        )
+        section[spot] = jnp.dot(taken, tconv[...], preferred_element_type=F32)
+
+    def activation_of(index, chunk, spot, target):
+        active[target] = activated(
+            section[spot] + bias_row,
+            frames[2 * index + 1, part_of(chunk)],
+            pick(first, index),
+            gain_row,
+            pick(limit, index),
+            columns,
+        )
+
+    def products_of(index, chunk, target):
+        products[index, :, part_of(chunk)] = lax.dot_general(
+            head[...], active[target], (((1,), (1,)), ((), ())), preferred_element_type=F32
+        )
+
+    def tap_block(index, k):
+        return products[index, k * taps : (k + 1) * taps]
+
+    arrive(0, 3)
+    units = [(index, chunk) for index in (2, 3, 1) for chunk in range(CHUNKS)]
+    before_frame_3, before_frame_1 = CHUNKS, 2 * CHUNKS
+    for step in range(len(units) + 2):
+        if step == before_frame_3:
+            arrive(4, 6)
+            pl.semaphore_wait(ready_sem.at[0], 5)
+            signal(ready_sem.at[1], y_device(2), y_device(-2), z_device(2), z_device(-2))
+        if step == before_frame_1:
+            arrive(11, 13)
+            pl.semaphore_wait(ready_sem.at[1], 4)
+            signal(ready_sem.at[2], other_core, x_device(1), x_device(2), x_device(-1))
+        if step < len(units):
+            section_of(*units[step], step % 2)
+        if 1 <= step < len(units) + 1:
+            activation_of(*units[step - 1], (step - 1) % 2, step % 2)
+        if step >= 2:
+            products_of(*units[step - 2], (step - 1) % 2)
+        if step == before_frame_1 + 1:
+            halo_out[0] = spatial_sum(
+                tap_block(frame_count - 2, 0) * pick(two, frame_count)
+                + tap_block(frame_count - 1, 1) * pick(one, frame_count),
+                latent_dim,
+                columns,
+            )
+            halo_out[1] = spatial_sum(
+                tap_block(frame_count - 1, 0) * pick(two, frame_count + 1), latent_dim, columns
+            )
+            halo = pltpu.make_async_remote_copy(
+                src_ref=halo_out,
+                dst_ref=halo_in,
+                send_sem=halo_sem.at[0],
+                recv_sem=halo_sem.at[1],
+                device_id=after,
+                device_id_type=MESH,
+            )
+            halo.start()
+
+    for chunk in range(CHUNKS):
+        part = part_of(chunk)
+        section[chunk % 2] = jnp.dot(
+            jnp.concatenate([frames[0, part], frames[1, part]], axis=1),
+            tconv[channels:, :],
+            preferred_element_type=F32,
+        )
+
+    latents[1] = spatial_sum(tap_block(1, 2), latent_dim, columns)
+    latents[2] = spatial_sum(tap_block(2, 2) + tap_block(1, 1) * pick(one, 2), latent_dim, columns)
+    latents[3] = spatial_sum(
+        tap_block(3, 2) + tap_block(2, 1) * pick(one, 3) + tap_block(1, 0) * pick(two, 3),
+        latent_dim,
+        columns,
+    )
+
+    arrive(14, 17)
     row = iota((total, 1), 0)
     owner, spot = lax.div(row, places), lax.rem(row, places)
     named = lax.div(owner, CORES) * shards + spot * CORES + lax.rem(owner, CORES)
@@ -229,110 +322,18 @@
     sooner = jnp.where(iota((tokens, tokens), 0) < iota((tokens, tokens), 1), 1.0, 0.0).astype(BF16)
     counts = jnp.dot(match[...], sooner, preferred_element_type=F32)
     rank = jnp.sum(jnp.where(matches, counts, 0.0), axis=0, keepdims=True)
-    bias_row = bias[...].reshape(1, channels)
-    gain_row = gain[...].reshape(1, channels)
     head_bias_column = column_of(head_bias[...])
     mean_column = column_of(mean[...])
     scale_column = column_of(scale[...])
 
-    pl.semaphore_wait(barrier, 1 + 1 + ALONG_X - 1 + along_y - 1 + replicas - 1)
-    rows = cells // CHUNKS
-    sends = []
     for chunk in range(CHUNKS):
-        part = pl.ds(chunk * rows, rows)
-        sends.append(
-            pltpu.make_async_remote_copy(
-                src_ref=frames_hbm.at[2 * frame_count - 1, part],
-                dst_ref=carried.at[part],
-                send_sem=carry_send.at[chunk],
-                recv_sem=carry_recv.at[chunk],
-                device_id=after,
-                device_id_type=MESH,
-            )
-        )
-        sends[-1].start()
-    signal(ready_sem, other_core)
-    for step in range(1, ALONG_X):
-        signal(ready_sem, x_device(step))
-
-    for load in loads[8:]:
-        load.wait()
-
-    def section_frame(index, carry):
-        taken = jnp.concatenate(
-            [frames[2 * index - 1], frames[2 * index], frames[2 * index + 1]], axis=1
-        )
-        section[...] = jnp.dot(taken, tconv[...], preferred_element_type=F32)
-        is_first, inside = pick(first, index), pick(limit, index)
-
-        def part_of(chunk, carry):
-            part = pl.ds(pl.multiple_of(chunk * rows, rows), rows)
-            active[part, :] = activated(
-                section[part, :] + bias_row,
-                frames[2 * index + 1, part, :],
-                is_first,
-                gain_row,
-                inside,
-                columns,
-            )
-            return carry
-
-        lax.fori_loop(0, CHUNKS, part_of, 0)
-        products[index] = lax.dot_general(
-            head[...], active[...], (((1,), (1,)), ((), ())), preferred_element_type=F32
-        )
-        return carry
-
-    lax.fori_loop(1, frame_count, section_frame, 0)
-
-    def tap_block(index, k):
-        return products[index, k * taps : (k + 1) * taps]
-
-    halo_out[0] = spatial_sum(
-        tap_block(frame_count - 2, 0) * pick(two, frame_count)
-        + tap_block(frame_count - 1, 1) * pick(one, frame_count),
-        latent_dim,
-        columns,
-    )
-    halo_out[1] = spatial_sum(
-        tap_block(frame_count - 1, 0) * pick(two, frame_count + 1), latent_dim, columns
-    )
-    halo = pltpu.make_async_remote_copy(
-        src_ref=halo_out,
-        dst_ref=halo_in,
-        send_sem=halo_sem.at[0],
-        recv_sem=halo_sem.at[1],
-        device_id=after,
-        device_id_type=MESH,
-    )
-    halo.start()
-
-    for index in range(1, frame_count):
-        block = tap_block(index, 2)
-        if index >= 2:
-            block = block + tap_block(index - 1, 1) * pick(one, index)
-        if index >= 3:
-            block = block + tap_block(index - 2, 0) * pick(two, index)
-        latents[index] = spatial_sum(block, latent_dim, columns)
-
-    section[...] = jnp.dot(
-        jnp.concatenate([frames[0], frames[1]], axis=1),
-        tconv[channels:, :],
-        preferred_element_type=F32,
-    )
-    is_first, inside = pick(first, 0), pick(limit, 0)
-    for chunk in range(CHUNKS):
-        part = pl.ds(chunk * rows, rows)
+        part = part_of(chunk)
         sends[chunk].wait_recv()
-        summed = section[part, :] + jnp.dot(
+        section[chunk % 2] += jnp.dot(
             carried[part, :], tconv[:channels, :], preferred_element_type=F32
         )
-        act = activated(
-            summed + bias_row, frames[1, part, :], is_first, gain_row, inside, columns
-        )
-        products[0, :, part] = lax.dot_general(
-            head[...], act, (((1,), (1,)), ((), ())), preferred_element_type=F32
-        )
+        activation_of(0, chunk, chunk % 2, chunk % 2)
+        products_of(0, chunk, chunk % 2)
 
     latents[0] = spatial_sum(tap_block(0, 2), latent_dim, columns)
     latents[1] += spatial_sum(tap_block(0, 1) * pick(one, 1), latent_dim, columns)
@@ -373,7 +374,7 @@
         match[...], ranked, (((1,), (1,)), ((), ())), preferred_element_type=F32
     ).astype(BF16)
 
-    pl.semaphore_wait(ready_sem, 1 + ALONG_X - 1)
+    pl.semaphore_wait(ready_sem.at[2], 4)
 
     def near_send(step, carry):
         index, device = near_device(step)
@@ -461,7 +462,7 @@
     exchanged = pltpu.VMEM((destinations, width), BF16)
     slots_out = pl.pallas_call(
         functools.partial(encode_kernel, replicas, places, height, columns),
-        out_shape=jax.ShapeDtypeStruct((destinations, width), F32),
+        out_shape=pltpu.VMEM((destinations, width), F32),
         in_specs=[pl.BlockSpec(memory_space=pltpu.HBM)] * len(operands),
         out_specs=pl.BlockSpec(memory_space=pltpu.VMEM),
         scratch_shapes=[
@@ -471,8 +472,8 @@
             pltpu.VMEM((cells, channels), BF16),
             pltpu.VMEM((2, latent_dim, cells), F32),
             pltpu.VMEM((2, latent_dim, cells), F32),
-            pltpu.VMEM((cells, channels), F32),
-            pltpu.VMEM((cells, channels), BF16),
+            pltpu.VMEM((2, cells // CHUNKS, channels), F32),
+            pltpu.VMEM((2, cells // CHUNKS, channels), BF16),
             pltpu.VMEM((frame_count, 27 * latent_dim, cells), F32),
             pltpu.VMEM((frame_count, latent_dim, cells), F32),
             pltpu.VMEM((destinations, tokens), BF16),
@@ -483,11 +484,11 @@
             exchanged,
             exchanged,
             exchanged,
-            pltpu.SemaphoreType.DMA((10 + frame_count,)),
+            pltpu.SemaphoreType.DMA((10 + 2 * frame_count,)),
             pltpu.SemaphoreType.DMA((CHUNKS,)),
             pltpu.SemaphoreType.DMA((CHUNKS,)),
             pltpu.SemaphoreType.DMA((2,)),
-            pltpu.SemaphoreType.REGULAR,
+            pltpu.SemaphoreType.REGULAR((3,)),
             pltpu.SemaphoreType.DMA((2,)),
             pltpu.SemaphoreType.DMA((2,)),
         ],

time: 42 us -> 35.8 us (0.85)
  Pallas kernels: 40.2 us -> 35 us
  other arithmetic: 1.62 us -> 0.67 us
    pallas_call x1, Pallas kernels: 40.2 us -> 35 us  [on_device(): pl.pallas_call(functools.partial(encode_kernel, replicas, places, height,...]
    reshape x1, other arithmetic: 1.62 us -> 0.67 us  [on_device(): return slots_out.astype(BF16).reshape(1, 1, destinations, width)]
where the time goes in v3:
time: 35.8 us; the launch traced here: 35.7 us
  Pallas kernels  35 us (98%)
  other arithmetic  0.67 us (2%)
    pallas_call x1, Pallas kernels, on_device(): pl.pallas_call(functools.partial(encode_kernel, replicas, places, height,...  35 us

profile of v3, /device:TPU:1, one launch (start us, length us, event | category | flops | bytes accessed | tf_op | source)
XLA Modules:
  0.0 35.7 jit_solution(6699114091449666959)
XLA Ops:
  0.0 35.0 %encode_and_route.1 = f32[512,128]{1,0:T(8,128)S(1)} custom-call(bf16[8,512,384]{2,1,0:T(8,128)(2,1)} %bitcast.11, s32[1,32]{1,0:T(1,128)} %clip_hbm.1, s32[1,32]{1,0:T(1,128)} %res_hbm.1, s32[1,512]{1,0:T(1,128)} %bitcast.14, bf16[1152,384]{1,0:T(8,128)(2,1)} %bitcast.12, f32[384]{0:T(512)} %bias_hbm.1, f32[384]{0:T(512)} %gain_hbm.1, ...), custom_call_target="tpu_custom_call" | custom-call | tf_op jit(solution)/shard_map/encode_and_route/pallas_call | solution.py:463
  35.0 0.7 %convert_bitcast_fusion = bf16[1,1,512,128]{3,2,1,0:T(8,128)(2,1)} fusion(f32[512,128]{1,0:T(8,128)S(1)} %encode_and_route.1), kind=kLoop, calls=%fused_computation | loop fusion | flops 65536 | bytes 393216 | tf_op jit(solution)/shard_map/reshape | solution.py:500

commit v4 on v3

--- a/solution.py
+++ b/solution.py
@@ -113,13 +113,8 @@
     products,
     latents,
     match,
-    turn,
-    back,
     unpatch,
     outgoing,
-    first_stage,
-    middle,
-    last_stage,
     load_sem,
     carry_send,
     carry_recv,
@@ -128,9 +123,9 @@
     send_sem,
     recv_sem,
 ):
-    near = replicas * CORES
-    total = near * places
     shards = places * CORES
+    total = replicas * shards
+    line = ALONG_X * CORES
     along_y = places // ALONG_X
     frame_count = frames.shape[0] // 2
     cells, channels = frames.shape[1:]
@@ -142,17 +137,9 @@
     core = lax.rem(shard, CORES)
     x = lax.rem(place, ALONG_X)
     y = lax.div(place, ALONG_X)
-    mine = replica * CORES + core
+    mine = replica * shards + shard
     after = (replica, lax.rem(shard + 1, shards))
     before = (replica, lax.rem(shard + shards - 1, shards))
-
-    def near_device(step):
-        index = lax.rem(mine + step, near)
-        return index, (lax.div(index, CORES), place * CORES + lax.rem(index, CORES))
-
-    def far_device(step):
-        index = lax.rem(place + step, places)
-        return index, (replica, index * CORES + core)
 
     def z_device(step):
         return (lax.rem(replica + step + replicas, replicas), shard)
@@ -195,13 +182,7 @@
         part = lax.rem(row, 2) * 2 + lax.rem(column, 2)
         return part * (cells // 4) + lax.div(row, 2) * (columns // 2) + lax.div(column, 2)
 
-    def slot(row):
-        rest = lax.rem(row, shards)
-        return lax.div(rest, CORES) * near + lax.div(row, shards) * CORES + lax.rem(rest, CORES)
-
     unpatch[...] = reorder(cells, patch_of)
-    turn[...] = reorder(total, lambda row: lax.rem(row, near) * places + lax.div(row, near))
-    back[...] = reorder(total, slot)
 
 
     rows = cells // CHUNKS
@@ -269,7 +250,7 @@
         if step == before_frame_1:
             arrive(11, 13)
             pl.semaphore_wait(ready_sem.at[1], 4)
-            signal(ready_sem.at[2], other_core, x_device(1), x_device(2), x_device(-1))
+            signal(ready_sem.at[2], other_core)
         if step < len(units):
             section_of(*units[step], step % 2)
         if 1 <= step < len(units) + 1:
@@ -277,6 +258,8 @@
         if step >= 2:
             products_of(*units[step - 2], (step - 1) % 2)
         if step == before_frame_1 + 1:
+            pl.semaphore_wait(ready_sem.at[2], 1)
+            signal(ready_sem.at[3], *[y_device(step) for step in range(1, along_y)])
             halo_out[0] = spatial_sum(
                 tap_block(frame_count - 2, 0) * pick(two, frame_count)
                 + tap_block(frame_count - 1, 1) * pick(one, frame_count),
@@ -313,11 +296,8 @@
     )
 
     arrive(14, 17)
-    row = iota((total, 1), 0)
-    owner, spot = lax.div(row, places), lax.rem(row, places)
-    named = lax.div(owner, CORES) * shards + spot * CORES + lax.rem(owner, CORES)
     tokens = dest.shape[1]
-    matches = dest[...] == named
+    matches = dest[...] == iota((total, 1), 0)
     match[...] = jnp.where(matches, 1.0, 0.0).astype(BF16)
     sooner = jnp.where(iota((tokens, tokens), 0) < iota((tokens, tokens), 1), 1.0, 0.0).astype(BF16)
     counts = jnp.dot(match[...], sooner, preferred_element_type=F32)
@@ -325,6 +305,9 @@
     head_bias_column = column_of(head_bias[...])
     mean_column = column_of(mean[...])
     scale_column = column_of(scale[...])
+
+    pl.semaphore_wait(ready_sem.at[3], along_y - 1)
+    signal(ready_sem.at[4], x_device(1), x_device(2), x_device(-1))
 
     for chunk in range(CHUNKS):
         part = part_of(chunk)
@@ -372,54 +355,43 @@
     ).astype(BF16)
     outgoing[...] = lax.dot_general(
         match[...], ranked, (((1,), (1,)), ((), ())), preferred_element_type=F32
-    ).astype(BF16)
-
-    pl.semaphore_wait(ready_sem.at[2], 4)
-
-    def near_send(step, carry):
-        index, device = near_device(step)
+    )
+
+    pl.semaphore_wait(ready_sem.at[4], ALONG_X - 1)
+
+    def send_row(to_replica, to_shard):
         pltpu.make_async_remote_copy(
-            src_ref=outgoing.at[pl.ds(index * places, places)],
-            dst_ref=first_stage.at[pl.ds(mine * places, places)],
-            send_sem=send_sem.at[0],
-            recv_sem=recv_sem.at[0],
-            device_id=device,
+            src_ref=outgoing.at[pl.ds(to_replica * shards + to_shard, 1)],
+            dst_ref=out_ref.at[pl.ds(mine, 1)],
+            send_sem=send_sem,
+            recv_sem=recv_sem,
+            device_id=(to_replica, to_shard),
             device_id_type=MESH,
         ).start()
-        return carry
-
-    lax.fori_loop(1, near, near_send, 0)
-    own = pl.ds(mine * places, places)
-    first_stage[own, :] = outgoing[own, :]
-    arrived = first_stage.at[pl.ds(0, (near - 1) * places)]
-    pltpu.make_async_copy(arrived, arrived, recv_sem.at[0]).wait()
-    middle[...] = jnp.dot(turn[...], first_stage[...], preferred_element_type=F32).astype(BF16)
-
-    def far_send(step, carry):
-        index, device = far_device(step)
-        pltpu.make_async_remote_copy(
-            src_ref=middle.at[pl.ds(index * near, near)],
-            dst_ref=last_stage.at[pl.ds(place * near, near)],
-            send_sem=send_sem.at[1],
-            recv_sem=recv_sem.at[1],
-            device_id=device,
-            device_id_type=MESH,
-        ).start()
-        return carry
-
-    lax.fori_loop(1, places, far_send, 0)
-    own = pl.ds(place * near, near)
-    last_stage[own, :] = middle[own, :]
-    for chunk in range(CHUNKS):
-        sends[chunk].wait_send()
+
+    def hops(offset):
+        far_z, far_y = offset
+        return min(far_z, replicas - far_z) + min(far_y, along_y - far_y)
+
+    offsets = [(far_z, far_y) for far_z in range(replicas) for far_y in range(along_y)]
+    for far_z, far_y in sorted(offsets, key=hops, reverse=True):
+        to_replica = lax.rem(replica + far_z, replicas)
+        to_line = lax.rem(y + far_y, along_y) * line
+
+        def send_line(step, carry, to_replica=to_replica, to_line=to_line):
+            send_row(to_replica, to_line + lax.rem(x * CORES + core + step, line))
+            return carry
+
+        lax.fori_loop(0 if far_z or far_y else 1, line, send_line, 0, unroll=True)
+
+    out_ref[pl.ds(mine, 1), :] = outgoing[pl.ds(mine, 1), :]
+    for send in sends:
+        send.wait_send()
     halo.wait_send()
-    sent = outgoing.at[pl.ds(0, (near - 1) * places)]
-    pltpu.make_async_copy(sent, sent, send_sem.at[0]).wait()
-    arrived = last_stage.at[pl.ds(0, (places - 1) * near)]
-    pltpu.make_async_copy(arrived, arrived, recv_sem.at[1]).wait()
-    out_ref[...] = jnp.dot(back[...], last_stage[...], preferred_element_type=F32)
-    sent = middle.at[pl.ds(0, (places - 1) * near)]
-    pltpu.make_async_copy(sent, sent, send_sem.at[1]).wait()
+    others = out_ref.at[pl.ds(0, total - 1)]
+    pltpu.make_async_copy(others, others, recv_sem).wait()
+    others = outgoing.at[pl.ds(0, total - 1)]
+    pltpu.make_async_copy(others, others, send_sem).wait()
 
 
 def on_device(
@@ -458,8 +430,6 @@
         latent_mean.reshape(1, latent_dim),
         latent_scale.reshape(1, latent_dim),
     )
-    square = pltpu.VMEM((destinations, destinations), BF16)
-    exchanged = pltpu.VMEM((destinations, width), BF16)
     slots_out = pl.pallas_call(
         functools.partial(encode_kernel, replicas, places, height, columns),
         out_shape=pltpu.VMEM((destinations, width), F32),
@@ -477,20 +447,15 @@
             pltpu.VMEM((frame_count, 27 * latent_dim, cells), F32),
             pltpu.VMEM((frame_count, latent_dim, cells), F32),
             pltpu.VMEM((destinations, tokens), BF16),
-            square,
-            square,
             pltpu.VMEM((cells, cells), BF16),
-            exchanged,
-            exchanged,
-            exchanged,
-            exchanged,
+            pltpu.VMEM((destinations, width), F32),
             pltpu.SemaphoreType.DMA((10 + 2 * frame_count,)),
             pltpu.SemaphoreType.DMA((CHUNKS,)),
             pltpu.SemaphoreType.DMA((CHUNKS,)),
             pltpu.SemaphoreType.DMA((2,)),
-            pltpu.SemaphoreType.REGULAR((3,)),
-            pltpu.SemaphoreType.DMA((2,)),
-            pltpu.SemaphoreType.DMA((2,)),
+            pltpu.SemaphoreType.REGULAR((5,)),
+            pltpu.SemaphoreType.DMA,
+            pltpu.SemaphoreType.DMA,
         ],
         compiler_params=pltpu.CompilerParams(
             collective_id=0, has_side_effects=True, vmem_limit_bytes=60 * 1024 * 1024

time: 35.8 us -> 35.5 us (level)
  no operation moved by 1% of the time
where the time goes in v4:
time: 35.5 us; the launch traced here: 35.4 us
  Pallas kernels  34.7 us (98%)
  other arithmetic  0.67 us (2%)
    pallas_call x1, Pallas kernels, on_device(): pl.pallas_call(functools.partial(encode_kernel, replicas, places, height,...  34.7 us

profile of v4, /device:TPU:1, one launch (start us, length us, event | category | flops | bytes accessed | tf_op | source)
XLA Modules:
  0.0 35.4 jit_solution(3807973964650151563)
XLA Ops:
  0.0 34.7 %encode_and_route.1 = f32[512,128]{1,0:T(8,128)S(1)} custom-call(bf16[8,512,384]{2,1,0:T(8,128)(2,1)} %bitcast.11, s32[1,32]{1,0:T(1,128)} %clip_hbm.1, s32[1,32]{1,0:T(1,128)} %res_hbm.1, s32[1,512]{1,0:T(1,128)} %bitcast.14, bf16[1152,384]{1,0:T(8,128)(2,1)} %bitcast.12, f32[384]{0:T(512)} %bias_hbm.1, f32[384]{0:T(512)} %gain_hbm.1, ...), custom_call_target="tpu_custom_call" | custom-call | tf_op jit(solution)/shard_map/encode_and_route/pallas_call | solution.py:433
  34.7 0.7 %convert_bitcast_fusion = bf16[1,1,512,128]{3,2,1,0:T(8,128)(2,1)} fusion(f32[512,128]{1,0:T(8,128)S(1)} %encode_and_route.1), kind=kLoop, calls=%fused_computation | loop fusion | flops 65536 | bytes 393216 | tf_op jit(solution)/shard_map/reshape | solution.py:465

commit v5 on v4

--- a/solution.py
+++ b/solution.py
@@ -114,18 +114,22 @@
     latents,
     match,
     unpatch,
+    pairing,
+    handed,
+    taken,
     outgoing,
     load_sem,
     carry_send,
     carry_recv,
     halo_sem,
     ready_sem,
+    swap_sem,
+    home_sem,
     send_sem,
     recv_sem,
 ):
     shards = places * CORES
     total = replicas * shards
-    line = ALONG_X * CORES
     along_y = places // ALONG_X
     frame_count = frames.shape[0] // 2
     cells, channels = frames.shape[1:]
@@ -137,7 +141,6 @@
     core = lax.rem(shard, CORES)
     x = lax.rem(place, ALONG_X)
     y = lax.div(place, ALONG_X)
-    mine = replica * shards + shard
     after = (replica, lax.rem(shard + 1, shards))
     before = (replica, lax.rem(shard + shards - 1, shards))
 
@@ -243,14 +246,16 @@
     units = [(index, chunk) for index in (2, 3, 1) for chunk in range(CHUNKS)]
     before_frame_3, before_frame_1 = CHUNKS, 2 * CHUNKS
     for step in range(len(units) + 2):
+        if step == 1:
+            pl.semaphore_wait(ready_sem.at[0], 5)
+            signal(ready_sem.at[1], y_device(2), y_device(-2), z_device(2), z_device(-2))
         if step == before_frame_3:
             arrive(4, 6)
-            pl.semaphore_wait(ready_sem.at[0], 5)
-            signal(ready_sem.at[1], y_device(2), y_device(-2), z_device(2), z_device(-2))
         if step == before_frame_1:
             arrive(11, 13)
+        if step == before_frame_1:
             pl.semaphore_wait(ready_sem.at[1], 4)
-            signal(ready_sem.at[2], other_core)
+            signal(ready_sem.at[2], *[y_device(step) for step in range(1, along_y)])
         if step < len(units):
             section_of(*units[step], step % 2)
         if 1 <= step < len(units) + 1:
@@ -258,8 +263,6 @@
         if step >= 2:
             products_of(*units[step - 2], (step - 1) % 2)
         if step == before_frame_1 + 1:
-            pl.semaphore_wait(ready_sem.at[2], 1)
-            signal(ready_sem.at[3], *[y_device(step) for step in range(1, along_y)])
             halo_out[0] = spatial_sum(
                 tap_block(frame_count - 2, 0) * pick(two, frame_count)
                 + tap_block(frame_count - 1, 1) * pick(one, frame_count),
@@ -297,17 +300,22 @@
 
     arrive(14, 17)
     tokens = dest.shape[1]
-    matches = dest[...] == iota((total, 1), 0)
+    chips = total // CORES
+    row = iota((total, 1), 0)
+    matches = dest[...] == jnp.where(row < chips, row * CORES + core, (row - chips) * CORES + 1 - core)
     match[...] = jnp.where(matches, 1.0, 0.0).astype(BF16)
     sooner = jnp.where(iota((tokens, tokens), 0) < iota((tokens, tokens), 1), 1.0, 0.0).astype(BF16)
     counts = jnp.dot(match[...], sooner, preferred_element_type=F32)
     rank = jnp.sum(jnp.where(matches, counts, 0.0), axis=0, keepdims=True)
+    column = iota((1, total), 1)
+    paired = jnp.where(column < chips, column * CORES + core, (column - chips) * CORES + 1 - core)
+    pairing[...] = jnp.where(row == paired, 1.0, 0.0).astype(BF16)
     head_bias_column = column_of(head_bias[...])
     mean_column = column_of(mean[...])
     scale_column = column_of(scale[...])
 
-    pl.semaphore_wait(ready_sem.at[3], along_y - 1)
-    signal(ready_sem.at[4], x_device(1), x_device(2), x_device(-1))
+    pl.semaphore_wait(ready_sem.at[2], along_y - 1)
+    signal(ready_sem.at[3], x_device(1), x_device(2), x_device(-1))
 
     for chunk in range(CHUNKS):
         part = part_of(chunk)
@@ -353,44 +361,68 @@
     ranked = jnp.concatenate(
         [jnp.where(rank == 0.0, features, 0.0), jnp.where(rank == 1.0, features, 0.0)], axis=0
     ).astype(BF16)
-    outgoing[...] = lax.dot_general(
-        match[...], ranked, (((1,), (1,)), ((), ())), preferred_element_type=F32
-    )
-
-    pl.semaphore_wait(ready_sem.at[4], ALONG_X - 1)
-
-    def send_row(to_replica, to_shard):
+    def routed(first_row):
+        return lax.dot_general(
+            match[first_row : first_row + chips],
+            ranked,
+            (((1,), (1,)), ((), ())),
+            preferred_element_type=F32,
+        ).astype(BF16)
+
+    handed[...] = routed(chips)
+    swap = pltpu.make_async_remote_copy(
+        src_ref=handed,
+        dst_ref=taken,
+        send_sem=swap_sem.at[0],
+        recv_sem=swap_sem.at[1],
+        device_id=other_core,
+        device_id_type=MESH,
+    )
+    swap.start()
+    kept = jnp.dot(pairing[:, :chips], routed(0), preferred_element_type=F32)
+    pl.semaphore_wait(ready_sem.at[3], ALONG_X - 1)
+    swap.wait_recv()
+    pairs = kept + jnp.dot(pairing[:, chips:], taken[...], preferred_element_type=F32)
+    outgoing[...] = pairs.astype(BF16).reshape(outgoing.shape)
+
+    mine = replica * places + place
+    home = pltpu.make_async_copy(outgoing.at[mine], out_ref.at[mine], home_sem)
+    home.start()
+
+    def hops(offset):
+        far_z, far_y, far_x = offset
+        return (
+            min(far_z, replicas - far_z) + min(far_y, along_y - far_y) + min(far_x, ALONG_X - far_x)
+        )
+
+    offsets = [
+        (far_z, far_y, far_x)
+        for far_z in range(replicas)
+        for far_y in range(along_y)
+        for far_x in range(ALONG_X)
+    ]
+    for far_z, far_y, far_x in sorted(offsets, key=hops, reverse=True):
+        if not far_z and not far_y and not far_x:
+            continue
+        to_replica = lax.rem(replica + far_z, replicas)
+        to_place = lax.rem(y + far_y, along_y) * ALONG_X + lax.rem(x + far_x, ALONG_X)
         pltpu.make_async_remote_copy(
-            src_ref=outgoing.at[pl.ds(to_replica * shards + to_shard, 1)],
-            dst_ref=out_ref.at[pl.ds(mine, 1)],
+            src_ref=outgoing.at[to_replica * places + to_place],
+            dst_ref=out_ref.at[mine],
             send_sem=send_sem,
             recv_sem=recv_sem,
-            device_id=(to_replica, to_shard),
+            device_id=(to_replica, to_place * CORES + core),
             device_id_type=MESH,
         ).start()
 
-    def hops(offset):
-        far_z, far_y = offset
-        return min(far_z, replicas - far_z) + min(far_y, along_y - far_y)
-
-    offsets = [(far_z, far_y) for far_z in range(replicas) for far_y in range(along_y)]
-    for far_z, far_y in sorted(offsets, key=hops, reverse=True):
-        to_replica = lax.rem(replica + far_z, replicas)
-        to_line = lax.rem(y + far_y, along_y) * line
-
-        def send_line(step, carry, to_replica=to_replica, to_line=to_line):
-            send_row(to_replica, to_line + lax.rem(x * CORES + core + step, line))
-            return carry
-
-        lax.fori_loop(0 if far_z or far_y else 1, line, send_line, 0, unroll=True)
-
-    out_ref[pl.ds(mine, 1), :] = outgoing[pl.ds(mine, 1), :]
+    home.wait()
+    swap.wait_send()
     for send in sends:
         send.wait_send()
     halo.wait_send()
-    others = out_ref.at[pl.ds(0, total - 1)]
+    others = out_ref.at[pl.ds(0, chips - 1)]
     pltpu.make_async_copy(others, others, recv_sem).wait()
-    others = outgoing.at[pl.ds(0, total - 1)]
+    others = outgoing.at[pl.ds(0, chips - 1)]
     pltpu.make_async_copy(others, others, send_sem).wait()
 
 
@@ -432,7 +464,7 @@
     )
     slots_out = pl.pallas_call(
         functools.partial(encode_kernel, replicas, places, height, columns),
-        out_shape=pltpu.VMEM((destinations, width), F32),
+        out_shape=pltpu.VMEM((destinations // CORES, CORES, width), BF16),
         in_specs=[pl.BlockSpec(memory_space=pltpu.HBM)] * len(operands),
         out_specs=pl.BlockSpec(memory_space=pltpu.VMEM),
         scratch_shapes=[
@@ -448,12 +480,17 @@
             pltpu.VMEM((frame_count, latent_dim, cells), F32),
             pltpu.VMEM((destinations, tokens), BF16),
             pltpu.VMEM((cells, cells), BF16),
-            pltpu.VMEM((destinations, width), F32),
+            pltpu.VMEM((destinations, destinations), BF16),
+            pltpu.VMEM((destinations // CORES, width), BF16),
+            pltpu.VMEM((destinations // CORES, width), BF16),
+            pltpu.VMEM((destinations // CORES, CORES, width), BF16),
             pltpu.SemaphoreType.DMA((10 + 2 * frame_count,)),
             pltpu.SemaphoreType.DMA((CHUNKS,)),
             pltpu.SemaphoreType.DMA((CHUNKS,)),
             pltpu.SemaphoreType.DMA((2,)),
-            pltpu.SemaphoreType.REGULAR((5,)),
+            pltpu.SemaphoreType.REGULAR((4,)),
+            pltpu.SemaphoreType.DMA((2,)),
+            pltpu.SemaphoreType.DMA,
             pltpu.SemaphoreType.DMA,
             pltpu.SemaphoreType.DMA,
         ],
@@ -462,7 +499,7 @@
         ),
         name="encode_and_route",
     )(*operands)
-    return slots_out.astype(BF16).reshape(1, 1, destinations, width)
+    return slots_out.reshape(1, 1, destinations, width)
 
 
 def solution(mesh):

time: 35.5 us -> 33.4 us (0.941)
  Pallas kernels: 34.7 us -> 32.6 us
  other arithmetic: 0.67 us -> 0 us
  local copies, waits for them, and re-layouts: 0 us -> 0.66 us
    pallas_call x1, Pallas kernels: 34.7 us -> 32.6 us  [on_device(): pl.pallas_call(functools.partial(encode_kernel, replicas, places, height,...]
    reshape x1 -> x0, other arithmetic: 0.67 us -> none  [on_device(): return slots_out.astype(BF16).reshape(1, 1, destinations, width)]
    unnamed x0 -> x1, local copies, waits for them, and re-layouts: none -> 0.66 us
where the time goes in v5:
time: 33.4 us; the launch traced here: 33.2 us
  Pallas kernels  32.6 us (98%)
  local copies, waits for them, and re-layouts  0.66 us (2%)
    pallas_call x1, Pallas kernels, on_device(): pl.pallas_call(functools.partial(encode_kernel, replicas, places, height,...  32.6 us

profile of v5, /device:TPU:1, one launch (start us, length us, event | category | flops | bytes accessed | tf_op | source)
XLA Modules:
  0.0 33.2 jit_solution(7379703631768123595)
XLA Ops:
  0.0 32.6 %encode_and_route.1 = bf16[256,2,128]{2,1,0:T(2,128)(2,1)S(1)} custom-call(bf16[8,512,384]{2,1,0:T(8,128)(2,1)} %bitcast.11, s32[1,32]{1,0:T(1,128)} %clip_hbm.1, s32[1,32]{1,0:T(1,128)} %res_hbm.1, s32[1,512]{1,0:T(1,128)} %bitcast.14, bf16[1152,384]{1,0:T(8,128)(2,1)} %bitcast.12, f32[384]{0:T(512)} %bias_hbm.1, f32[384]{0:T(512)} %gain_hbm.1, ...), custom_call_target="tpu_custom_call" | custom-call | tf_op jit(solution)/shard_map/encode_and_route/pallas_call | solution.py:465
  32.6 0.7 %copy.13 = bf16[1,1,512,128]{3,2,1,0:T(8,128)(2,1)} copy(bf16[1,1,512,128]{3,2,1,0:T(8,128)(2,1)S(1)} %bitcast.10) | data formatting | bytes 262144

commit v6 on v5

--- a/solution.py
+++ b/solution.py
@@ -114,7 +114,7 @@
     latents,
     match,
     unpatch,
-    pairing,
+    dest_other,
     handed,
     taken,
     outgoing,
@@ -161,32 +161,26 @@
         for device in devices:
             pl.semaphore_signal(semaphore, inc=1, device_id=device, device_id_type=MESH)
 
-    signal(barrier, before, other_core, x_device(1), x_device(-1))
-    signal(barrier, y_device(1), y_device(-1), z_device(1), z_device(-1))
-
     wanted = [(tconv_hbm, tconv)]
-    wanted += [(frames_hbm.at[index], frames.at[index]) for index in (3, 4, 5, 6, 7)]
-    wanted += [(head_hbm, head), (bias_hbm, bias), (gain_hbm, gain), (clip_hbm, clip), (res_hbm, res)]
-    wanted += [(frames_hbm.at[index], frames.at[index]) for index in (2, 1, 0)]
+    wanted += [(frames_hbm.at[pl.ds(3, 3)], frames.at[pl.ds(3, 3)])]
+    wanted += [(frames_hbm.at[pl.ds(6, 2)], frames.at[pl.ds(6, 2)]), (head_hbm, head)]
+    wanted += [(clip_hbm, clip), (res_hbm, res), (bias_hbm, bias), (gain_hbm, gain)]
     wanted += [(dest_hbm, dest), (head_bias_hbm, head_bias), (mean_hbm, mean), (scale_hbm, scale)]
+    wanted += [(frames_hbm.at[pl.ds(0, 3)], frames.at[pl.ds(0, 3)])]
     loads = [
         pltpu.make_async_copy(source, target, load_sem.at[index])
         for index, (source, target) in enumerate(wanted)
     ]
-    for load in loads:
+    for load in loads[:2]:
+        load.start()
+    signal(barrier, before, other_core, x_device(1), x_device(-1))
+    signal(barrier, y_device(1), y_device(-1), z_device(1), z_device(-1))
+    for load in loads[2:]:
         load.start()
 
     def arrive(first_load, last_load):
         for load in loads[first_load : last_load + 1]:
             load.wait()
-
-    def patch_of(cell):
-        row, column = lax.div(cell, columns), lax.rem(cell, columns)
-        part = lax.rem(row, 2) * 2 + lax.rem(column, 2)
-        return part * (cells // 4) + lax.div(row, 2) * (columns // 2) + lax.div(column, 2)
-
-    unpatch[...] = reorder(cells, patch_of)
-
 
     rows = cells // CHUNKS
     sends = [
@@ -205,7 +199,17 @@
         send.start()
     signal(ready_sem.at[0], x_device(1), y_device(1), y_device(-1), z_device(1), z_device(-1))
 
-    arrive(7, 10)
+    asked = pltpu.make_async_remote_copy(
+        src_ref=dest_hbm,
+        dst_ref=dest_other,
+        send_sem=swap_sem.at[0],
+        recv_sem=swap_sem.at[1],
+        device_id=other_core,
+        device_id_type=MESH,
+    )
+    asked.start()
+
+    arrive(4, 7)
     first_frame = shard * frame_count
     first, one, two, limit = frame_facts(
         clip[...].astype(F32), res[...].astype(F32), first_frame, shards * frame_count, columns
@@ -242,7 +246,7 @@
     def tap_block(index, k):
         return products[index, k * taps : (k + 1) * taps]
 
-    arrive(0, 3)
+    arrive(0, 1)
     units = [(index, chunk) for index in (2, 3, 1) for chunk in range(CHUNKS)]
     before_frame_3, before_frame_1 = CHUNKS, 2 * CHUNKS
     for step in range(len(units) + 2):
@@ -250,10 +254,10 @@
             pl.semaphore_wait(ready_sem.at[0], 5)
             signal(ready_sem.at[1], y_device(2), y_device(-2), z_device(2), z_device(-2))
         if step == before_frame_3:
-            arrive(4, 6)
+            arrive(2, 3)
         if step == before_frame_1:
-            arrive(11, 13)
-        if step == before_frame_1:
+            arrive(12, 12)
+        if step == 5:
             pl.semaphore_wait(ready_sem.at[1], 4)
             signal(ready_sem.at[2], *[y_device(step) for step in range(1, along_y)])
         if step < len(units):
@@ -298,24 +302,31 @@
         columns,
     )
 
-    arrive(14, 17)
+    def patch_of(cell):
+        row, column = lax.div(cell, columns), lax.rem(cell, columns)
+        part = lax.rem(row, 2) * 2 + lax.rem(column, 2)
+        return part * (cells // 4) + lax.div(row, 2) * (columns // 2) + lax.div(column, 2)
+
+    unpatch[...] = reorder(cells, patch_of)
+
     tokens = dest.shape[1]
     chips = total // CORES
     row = iota((total, 1), 0)
-    matches = dest[...] == jnp.where(row < chips, row * CORES + core, (row - chips) * CORES + 1 - core)
+    source = lax.rem(row, CORES)
+    from_here = source == core
+    arrive(8, 11)
+    asked.wait_recv()
+    matches = jnp.where(from_here, dest[...], dest_other[...]) == row - source + core
     match[...] = jnp.where(matches, 1.0, 0.0).astype(BF16)
-    sooner = jnp.where(iota((tokens, tokens), 0) < iota((tokens, tokens), 1), 1.0, 0.0).astype(BF16)
-    counts = jnp.dot(match[...], sooner, preferred_element_type=F32)
-    rank = jnp.sum(jnp.where(matches, counts, 0.0), axis=0, keepdims=True)
-    column = iota((1, total), 1)
-    paired = jnp.where(column < chips, column * CORES + core, (column - chips) * CORES + 1 - core)
-    pairing[...] = jnp.where(row == paired, 1.0, 0.0).astype(BF16)
+    token = iota((1, tokens), 1).astype(F32)
+    soonest = jnp.min(jnp.where(matches, token, float(tokens)), axis=1, keepdims=True)
+    second = jnp.where(matches & (token != soonest), 1.0, 0.0)
+    rank = jnp.sum(jnp.where(from_here, second, 0.0), axis=0, keepdims=True)
+    rank_other = jnp.sum(jnp.where(from_here, 0.0, second), axis=0, keepdims=True)
     head_bias_column = column_of(head_bias[...])
     mean_column = column_of(mean[...])
     scale_column = column_of(scale[...])
 
-    pl.semaphore_wait(ready_sem.at[2], along_y - 1)
-    signal(ready_sem.at[3], x_device(1), x_device(2), x_device(-1))
 
     for chunk in range(CHUNKS):
         part = part_of(chunk)
@@ -325,6 +336,9 @@
         )
         activation_of(0, chunk, chunk % 2, chunk % 2)
         products_of(0, chunk, chunk % 2)
+        if chunk == 0:
+            pl.semaphore_wait(ready_sem.at[2], along_y - 1)
+            signal(ready_sem.at[3], x_device(1), x_device(2), x_device(-1))
 
     latents[0] = spatial_sum(tap_block(0, 2), latent_dim, columns)
     latents[1] += spatial_sum(tap_block(0, 1) * pick(one, 1), latent_dim, columns)
@@ -358,31 +372,29 @@
         ],
         axis=0,
     )
-    ranked = jnp.concatenate(
-        [jnp.where(rank == 0.0, features, 0.0), jnp.where(rank == 1.0, features, 0.0)], axis=0
-    ).astype(BF16)
-    def routed(first_row):
-        return lax.dot_general(
-            match[first_row : first_row + chips],
-            ranked,
-            (((1,), (1,)), ((), ())),
-            preferred_element_type=F32,
-        ).astype(BF16)
-
-    handed[...] = routed(chips)
+    handed[...] = features.astype(BF16)
     swap = pltpu.make_async_remote_copy(
         src_ref=handed,
         dst_ref=taken,
-        send_sem=swap_sem.at[0],
-        recv_sem=swap_sem.at[1],
+        send_sem=swap_sem.at[2],
+        recv_sem=swap_sem.at[3],
         device_id=other_core,
         device_id_type=MESH,
     )
     swap.start()
-    kept = jnp.dot(pairing[:, :chips], routed(0), preferred_element_type=F32)
+
+    def routed(values, ranks):
+        ranked = jnp.concatenate(
+            [jnp.where(ranks == 0.0, values, 0.0), jnp.where(ranks == 1.0, values, 0.0)], axis=0
+        ).astype(BF16)
+        return lax.dot_general(
+            match[...], ranked, (((1,), (1,)), ((), ())), preferred_element_type=F32
+        )
+
+    kept = routed(features, rank)
     pl.semaphore_wait(ready_sem.at[3], ALONG_X - 1)
     swap.wait_recv()
-    pairs = kept + jnp.dot(pairing[:, chips:], taken[...], preferred_element_type=F32)
+    pairs = jnp.where(from_here, kept, routed(taken[...].astype(F32), rank_other))
     outgoing[...] = pairs.astype(BF16).reshape(outgoing.shape)
 
     mine = replica * places + place
@@ -416,6 +428,7 @@
         ).start()
 
     home.wait()
+    asked.wait_send()
     swap.wait_send()
     for send in sends:
         send.wait_send()
@@ -480,16 +493,16 @@
             pltpu.VMEM((frame_count, latent_dim, cells), F32),
             pltpu.VMEM((destinations, tokens), BF16),
             pltpu.VMEM((cells, cells), BF16),
-            pltpu.VMEM((destinations, destinations), BF16),
-            pltpu.VMEM((destinations // CORES, width), BF16),
-            pltpu.VMEM((destinations // CORES, width), BF16),
+            pltpu.VMEM((1, tokens), jnp.int32),
+            pltpu.VMEM((4 * latent_dim, tokens), BF16),
+            pltpu.VMEM((4 * latent_dim, tokens), BF16),
             pltpu.VMEM((destinations // CORES, CORES, width), BF16),
-            pltpu.SemaphoreType.DMA((10 + 2 * frame_count,)),
+            pltpu.SemaphoreType.DMA((13,)),
             pltpu.SemaphoreType.DMA((CHUNKS,)),
             pltpu.SemaphoreType.DMA((CHUNKS,)),
             pltpu.SemaphoreType.DMA((2,)),
             pltpu.SemaphoreType.REGULAR((4,)),
-            pltpu.SemaphoreType.DMA((2,)),
+            pltpu.SemaphoreType.DMA((4,)),
             pltpu.SemaphoreType.DMA,
             pltpu.SemaphoreType.DMA,
             pltpu.SemaphoreType.DMA,

time: 33.4 us -> 33.2 us (level)
  no operation moved by 1% of the time
where the time goes in v6:
time: 33.2 us; the launch traced here: 33 us
  Pallas kernels  32.4 us (98%)
  local copies, waits for them, and re-layouts  0.66 us (2%)
    pallas_call x1, Pallas kernels, on_device(): pl.pallas_call(functools.partial(encode_kernel, replicas, places, height,...  32.4 us

profile of v6, /device:TPU:1, one launch (start us, length us, event | category | flops | bytes accessed | tf_op | source)
XLA Modules:
  0.0 33.0 jit_solution(6846625085512372964)
XLA Ops:
  0.0 32.4 %encode_and_route.1 = bf16[256,2,128]{2,1,0:T(2,128)(2,1)S(1)} custom-call(bf16[8,512,384]{2,1,0:T(8,128)(2,1)} %bitcast.11, s32[1,32]{1,0:T(1,128)} %clip_hbm.1, s32[1,32]{1,0:T(1,128)} %res_hbm.1, s32[1,512]{1,0:T(1,128)} %bitcast.14, bf16[1152,384]{1,0:T(8,128)(2,1)} %bitcast.12, f32[384]{0:T(512)} %bias_hbm.1, f32[384]{0:T(512)} %gain_hbm.1, ...), custom_call_target="tpu_custom_call" | custom-call | tf_op jit(solution)/shard_map/encode_and_route/pallas_call | solution.py:478
  32.4 0.7 %copy.13 = bf16[1,1,512,128]{3,2,1,0:T(8,128)(2,1)} copy(bf16[1,1,512,128]{3,2,1,0:T(8,128)(2,1)S(1)} %bitcast.10) | data formatting | bytes 262144

commit v7 on v5

--- a/solution.py
+++ b/solution.py
@@ -304,9 +304,9 @@
     row = iota((total, 1), 0)
     matches = dest[...] == jnp.where(row < chips, row * CORES + core, (row - chips) * CORES + 1 - core)
     match[...] = jnp.where(matches, 1.0, 0.0).astype(BF16)
-    sooner = jnp.where(iota((tokens, tokens), 0) < iota((tokens, tokens), 1), 1.0, 0.0).astype(BF16)
-    counts = jnp.dot(match[...], sooner, preferred_element_type=F32)
-    rank = jnp.sum(jnp.where(matches, counts, 0.0), axis=0, keepdims=True)
+    token = iota((1, tokens), 1).astype(F32)
+    soonest = jnp.min(jnp.where(matches, token, float(tokens)), axis=1, keepdims=True)
+    rank = jnp.sum(jnp.where(matches & (token != soonest), 1.0, 0.0), axis=0, keepdims=True)
     column = iota((1, total), 1)
     paired = jnp.where(column < chips, column * CORES + core, (column - chips) * CORES + 1 - core)
     pairing[...] = jnp.where(row == paired, 1.0, 0.0).astype(BF16)
@@ -395,13 +395,17 @@
             min(far_z, replicas - far_z) + min(far_y, along_y - far_y) + min(far_x, ALONG_X - far_x)
         )
 
+    def spread(offset):
+        far_z, far_y, far_x = offset
+        return hops(offset), (far_z * 37 + far_y * 23 + far_x * 11) % 64
+
     offsets = [
         (far_z, far_y, far_x)
         for far_z in range(replicas)
         for far_y in range(along_y)
         for far_x in range(ALONG_X)
     ]
-    for far_z, far_y, far_x in sorted(offsets, key=hops, reverse=True):
+    for far_z, far_y, far_x in sorted(offsets, key=spread, reverse=True):
         if not far_z and not far_y and not far_x:
             continue
         to_replica = lax.rem(replica + far_z, replicas)

time: 33.4 us -> 33.6 us (level)
  no operation moved by 1% of the time
where the time goes in v7:
time: 33.6 us; the launch traced here: 33.5 us
  Pallas kernels  32.8 us (98%)
  local copies, waits for them, and re-layouts  0.66 us (2%)
    pallas_call x1, Pallas kernels, on_device(): pl.pallas_call(functools.partial(encode_kernel, replicas, places, height,...  32.8 us

profile of v7, /device:TPU:1, one launch (start us, length us, event | category | flops | bytes accessed | tf_op | source)
XLA Modules:
  0.0 33.5 jit_solution(12611602042990238771)
XLA Ops:
  0.0 32.8 %encode_and_route.1 = bf16[256,2,128]{2,1,0:T(2,128)(2,1)S(1)} custom-call(bf16[8,512,384]{2,1,0:T(8,128)(2,1)} %bitcast.11, s32[1,32]{1,0:T(1,128)} %clip_hbm.1, s32[1,32]{1,0:T(1,128)} %res_hbm.1, s32[1,512]{1,0:T(1,128)} %bitcast.14, bf16[1152,384]{1,0:T(8,128)(2,1)} %bitcast.12, f32[384]{0:T(512)} %bias_hbm.1, f32[384]{0:T(512)} %gain_hbm.1, ...), custom_call_target="tpu_custom_call" | custom-call | tf_op jit(solution)/shard_map/encode_and_route/pallas_call | solution.py:469
  32.8 0.7 %copy.13 = bf16[1,1,512,128]{3,2,1,0:T(8,128)(2,1)} copy(bf16[1,1,512,128]{3,2,1,0:T(8,128)(2,1)S(1)} %bitcast.10) | data formatting | bytes 262144
